TPU v7x, 32 devices: a whole 2x2x4 slice. The times are simulated.
32 devices in a mesh: wide: 8 (over y, x, core), narrow: 4 (over z).
Axes of the slice: x: 2, y: 2, z: 4, core: 2. Of those that a mesh axis runs over, the one named last changes fastest.
Arguments:
- tokens: bfloat16 [8, 2048, 768], P('wide', 'narrow'), may hold values from -6 to 6
- segment: int32 [8, 2048], P('wide'), may hold values from 0 to 10, as said below
- padding: int32 [8, 2048], P('wide'), may hold values from 0 to 1, as said below
- coords: int32 [2, 8, 2048], P(None, 'wide'), may hold values from 0 to 23, as said below
- ln1_gain: float32 [768], replicated, may hold values from 0.5 to 1.5
- ln1_shift: float32 [768], replicated, may hold values from -1 to 1
- query_key_value_weight: bfloat16 [768, 2304], replicated, may hold values from -0.21875 to 0.21875
- b_qkv: float32 [2304], replicated, may hold values from -3 to 3
- output_weight: bfloat16 [768, 768], replicated, may hold values from -0.875 to 0.875
- b_out: float32 [768], replicated, may hold values from -3 to 3
- rope_freqs: float32 [2, 12, 32], replicated, may hold values from -3 to 3
- ln2_gain: float32 [768], replicated, may hold values from 0.5 to 1.5
- ln2_shift: float32 [768], replicated, may hold values from -1 to 1
- w_up: bfloat16 [768, 3072], P(None, 'narrow'), may hold values from -0.21875 to 0.21875
- b_up: float32 [3072], P('narrow'), may hold values from -3 to 3
- w_down: bfloat16 [3072, 768], P('narrow')
- b_down: float32 [768], replicated, may hold values from -3 to 3
- cotangent: bfloat16 [8, 2048, 768], P('wide', 'narrow'), may hold values from -6 to 6
Outputs:
- activations: bfloat16 [8, 2048, 768], P('wide', 'narrow')
- input_grad: float32 [8, 2048, 768], P('wide', 'narrow')
- grad_ln1_gain: float32 [768], replicated
- grad_ln1_shift: float32 [768], replicated
- grad_w_qkv: float32 [768, 2304], replicated
- grad_b_qkv: float32 [2304], replicated
- grad_w_out: float32 [768, 768], replicated
- grad_b_out: float32 [768], replicated
- grad_freqs: float32 [2, 12, 32], replicated
- grad_ln2_gain: float32 [768], replicated
- grad_ln2_shift: float32 [768], replicated
- grad_w_up: float32 [768, 3072], P(None, 'narrow')
- grad_b_up: float32 [3072], P('narrow')
- grad_w_down: float32 [3072, 768], P('narrow')
- grad_b_down: float32 [768], replicated
- rot_sq: float32 [], replicated
- other_sq: float32 [], replicated
Inputs may be any that keep to these rules, and one draw needn't show every extreme that they name: `segment`: each sequence packs whole images of 14, 20 or 24 patches on a side in order while they fit; slots of one image carry its number, counted from 0; padding slots at the end carry the number after the last image. One sequence holds only 14-side images. `padding`: 1 exactly on the slots after the last image of a sequence. `coords`: row and column of a patch in its image, row by row; 0 on padding.
All inputs are finite; a program needn't handle non-finite values.
Results may differ from a plain program's by a relative error of at most 0.009.
The roundings to bfloat16 on the way count: a program that leaves them out, or rounds other values in their place, can miss the bound.
Values may be sent and summed in bfloat16 or wider, within the bound.
No kernel may reach another device: no remote copies, remote signals or barrier semaphores. Data moves between devices by JAX's collectives and lax.ppermute only.
A program may use at most 384 MiB of HBM per device.

v0:
```python
import functools

import jax
import jax.numpy as jnp
import numpy as np
from jax import lax
from jax.experimental import pallas as pl
from jax.experimental.pallas import tpu as pltpu
from jax.sharding import Mesh, PartitionSpec as P

EPS = 1e-06
MASKED = -1e30
BLK = 128
SPAN = 6
SPAN_SIDE = 3
SPAN_BACK = 2
GROUP = 4
REACH = 64
STAT_ROWS = 6
STAT_PAD = 16
SIDE = 32
LN1_GAIN, LN1_SHIFT, B_OUT, LN2_GAIN, LN2_SHIFT, B_DOWN = (slice(n, n + 1) for n in range(6))
LOG2E = np.float32(1.4426950408889634)
BF = jnp.bfloat16
F32 = jnp.float32
PLANE = ("a", "b", "c")
SWAP = [(0, 1), (1, 0)]
FIRST = [(i, i ^ (4 if i % 2 else 2)) for i in range(8)]
SECOND = [(i, i ^ (2 if i % 2 else 4)) for i in range(8)]


def dot(left, right):
    return lax.dot_general(left, right, (((1,), (0,)), ((), ())), preferred_element_type=F32)


def dot_nt(left, right):
    return lax.dot_general(left, right, (((1,), (1,)), ((), ())), preferred_element_type=F32)


def dot_tn(left, right):
    return lax.dot_general(left, right, (((0,), (0,)), ((), ())), preferred_element_type=F32)


def params(mebibytes):
    return pltpu.CompilerParams(vmem_limit_bytes=mebibytes * 1024 * 1024)


def cost(us):
    return pl.CostEstimate(
        flops=int(us * 1.15e9), bytes_accessed=int(us * 3.0e6), transcendentals=0
    )


def whole(shape):
    return pl.BlockSpec(shape, lambda *_: (0,) * len(shape))


ANY = pl.BlockSpec(memory_space=pl.ANY)
SMEM = pl.BlockSpec(memory_space=pltpu.SMEM)


def rounded(x):
    return lax.reduce_precision(x, exponent_bits=8, mantissa_bits=7)


def turn_table(rope_freqs):
    lanes = rope_freqs.shape[1] * rope_freqs.shape[2]
    freq = rope_freqs.reshape(2, 1, lanes)
    angle = jnp.arange(SIDE, dtype=F32)[None, :, None] * freq
    cosine, sine = jnp.cos(angle), jnp.sin(angle)

    def halves(x):
        return jnp.concatenate([x.astype(BF), (x - rounded(x)).astype(BF)], 0)

    def grouped(x):
        return x.reshape(2 * SIDE, lanes // 128, 1, 128)

    zero = jnp.zeros((2 * SIDE, lanes // 128, 2, 128), BF)
    rows = jnp.concatenate([grouped(halves(cosine[0])), grouped(halves(sine[0])), zero], 2)
    cols = jnp.concatenate([zero, grouped(halves(cosine[1])), grouped(halves(sine[1]))], 2)
    return jnp.concatenate([rows, cols], 0).reshape(4 * SIDE, 4 * lanes)


def cos_sin(onehot, table):
    parts = dot(onehot, table)
    cr, sr, cc, sc = (parts[:, lanes_of(n, 128)] for n in range(4))
    return cr * cc - sr * sc, sr * cc + cr * sc


def layer_norm_low(x, gain, shift):
    centred = x - jnp.mean(x, -1, keepdims=True)
    var = jnp.mean(centred * centred, -1, keepdims=True)
    return (centred * lax.rsqrt(var + EPS) * gain + shift).astype(BF)


def project(norm, hot_ref, table_ref, weights, b_ref, outs, exact=()):
    width = norm.shape[1]
    for g in range(width // 256):
        c, s = cos_sin(hot_ref[...], table_ref[:, lanes_of(g, 512)])
        for n, out in outs:
            lo = n * width + 256 * g
            proj = dot(norm, weights[:, lo : lo + 256]) + b_ref[:, lo : lo + 256]
            if n == 2:
                out[:, lanes_of(g)] = proj.astype(BF)
                continue
            for half, turned in enumerate(
                (proj[:, :128] * c - proj[:, 128:] * s, proj[:, :128] * s + proj[:, 128:] * c)
            ):
                at = slice(256 * g + 128 * half, 256 * g + 128 * half + 128)
                out[:, at] = turned.astype(BF)
                if exact:
                    exact[n][:, at] = turned


def qkv_own_kernel(
    x_ref, hot_ref, vec_ref, w_ref, b_ref, order_ref, table_ref,
    q_ref, k_ref, v_ref, pq_ref, pk_ref, w_turned,
):
    width = x_ref.shape[1]

    @pl.when(pl.program_id(0) == 0)
    def _():
        for g in range(2 * width // 256):
            at = slice(256 * g, 256 * g + 256)
            w_turned[:, at] = dot(w_ref[:, at], order_ref[...]).astype(BF)
        w_turned[:, 2 * width :] = w_ref[:, 2 * width :]

    norm = layer_norm_low(x_ref[...].astype(F32), vec_ref[LN1_GAIN], vec_ref[LN1_SHIFT])
    outs = [(0, q_ref), (1, k_ref), (2, v_ref)]
    project(norm, hot_ref, table_ref, w_turned, b_ref, outs, (pq_ref, pk_ref))


def qkv_own_call(x, onehot, vectors, weight, bias, order, table, first):
    own, width = x.shape
    rows = onehot.shape[0]
    tile = 256
    shape = jax.ShapeDtypeStruct((rows, width), BF)
    exact = jax.ShapeDtypeStruct((own, width), F32)
    row = lambda w: pl.BlockSpec((tile, w), lambda i: (i, 0))
    inside = lambda w: pl.BlockSpec(
        (pl.Element(tile), pl.Element(w)), lambda i: (pl.multiple_of(first + tile * i, BLK), 0)
    )
    return pl.pallas_call(
        qkv_own_kernel,
        grid=(own // tile,),
        in_specs=[
            row(width),
            inside(onehot.shape[1]),
            whole(vectors.shape),
            whole(weight.shape),
            whole((1, 3 * width)),
            whole(order.shape),
            whole(table.shape),
        ],
        out_specs=[inside(width)] * 3 + [row(width)] * 2 + [whole(weight.shape)],
        out_shape=[shape] * 3 + [exact] * 2 + [jax.ShapeDtypeStruct(weight.shape, BF)],
        compiler_params=params(56),
        cost_estimate=cost(8),
        name="qkv_own",
    )(x, onehot, vectors, weight, bias[None], order, table)


def halo_kernel(
    far_l, near_l, near_r, far_r, hot_ref, vec_ref, w_ref, b_ref, table_ref, *refs, which
):
    refs = refs[len(which) :]
    out_refs, (x_all, sem) = refs[: len(which)], refs[len(which) :]
    width = x_all.shape[1]
    step = pl.program_id(0)
    tile = out_refs[0].shape[0]

    @pl.when(step == 0)
    def _():
        own, reach = near_l.shape[0], far_l.shape[0]
        total = x_all.shape[0]
        blank = total // 2 - own - reach
        copies = []
        at = blank
        for n, ref in enumerate((far_l, near_l, near_r, far_r)):
            copies.append(
                pltpu.make_async_copy(ref, x_all.at[at : at + ref.shape[0], :], sem.at[n])
            )
            copies[-1].start()
            at += ref.shape[0]
        x_all[:blank, :] = jnp.zeros((blank, width), BF)
        x_all[total - blank :, :] = jnp.zeros((blank, width), BF)
        for copy in copies:
            copy.wait()

    x = x_all[pl.ds(pl.multiple_of(step * tile, tile), tile), :].astype(F32)
    norm = layer_norm_low(x, vec_ref[LN1_GAIN], vec_ref[LN1_SHIFT])
    project(norm, hot_ref, table_ref, w_ref, b_ref, list(zip(which, out_refs)))


def halo_call(pieces, onehot, vectors, weight, bias, table, arrays, which, first):
    rows, width = arrays[0].shape
    own = pieces[1].shape[0]
    tile = first // 2
    at = lambda w: pl.BlockSpec(
        (pl.Element(tile), pl.Element(w)),
        lambda i: (pl.multiple_of(tile * i + jnp.where(i >= 2, own, 0), 64), 0),
    )
    return pl.pallas_call(
        functools.partial(halo_kernel, which=which),
        grid=(4,),
        in_specs=[ANY] * 4
        + [
            at(onehot.shape[1]),
            whole(vectors.shape),
            whole(weight.shape),
            whole((1, 3 * width)),
            whole(table.shape),
        ]
        + [ANY] * len(which),
        out_specs=[at(width)] * len(which),
        out_shape=[jax.ShapeDtypeStruct((rows, width), BF)] * len(which),
        input_output_aliases={9 + n: n for n in range(len(which))},
        scratch_shapes=[pltpu.VMEM((2 * first, width), BF), pltpu.SemaphoreType.DMA((4,))],
        compiler_params=params(56),
        cost_estimate=cost(4 * len(which)),
        name="halo",
    )(*pieces, onehot, vectors, weight, bias[None], table, *arrays)


def head_stack(block, turned, scale=None):
    lane = lax.broadcasted_iota(jnp.int32, block.shape, 1)
    head = (lane % 128) // 32 if turned else lane // 64
    if scale is not None:
        block = block * scale
    zero = jnp.zeros_like(block)
    return jnp.concatenate([jnp.where(head == h, block, zero) for h in range(GROUP)], 0)


def fold8(x, op):
    return op(x.reshape(x.shape[0] // 8, 8, x.shape[1]), axis=0)


def key_span(ident_ref, ident_q, start, c, span, end):
    block = jnp.minimum(start + c * span, end - span)
    lower = (start + c * span - block) * BLK
    at = pl.ds(pl.multiple_of(block * BLK, BLK), span * BLK)
    row = lax.broadcasted_iota(jnp.int32, (span * BLK, BLK), 0)
    return at, (ident_ref[at, :] == ident_q) & (row >= lower)


def lanes_of(g, size=256):
    return slice(size * g, size * g + size)


def forward_kernel(
    bound_ref, q_ref, k_ref, v_ref, idk_ref, idq_ref, *refs, first, base
):
    o_ref, low_ref, lse_ref, s_ref, acc_ref, q4_ref = refs[-6:]
    i = pl.program_id(0) + base
    groups = k_ref.shape[1] // 256
    lanes = GROUP * BLK
    window = k_ref.shape[0] // BLK
    start, count = bound_ref[i, 0], bound_ref[i, 1]
    for g in range(groups):
        q4_ref[g] = head_stack(q_ref[:, lanes_of(g)], True, jnp.asarray(0.125, BF))
    ident_q = idq_ref[pl.ds(first // BLK + i, 1), :]

    def scores(c, top):
        at, seen = key_span(idk_ref, ident_q, start, c, SPAN, window)
        here = pl.ds(pl.multiple_of(c * SPAN * BLK, BLK), SPAN * BLK)
        tops = []
        for g in range(groups):
            s = dot_nt(k_ref[at, lanes_of(g)], q4_ref[g]) * LOG2E
            for h in range(GROUP):
                masked = jnp.where(seen, s[:, lanes_of(h, BLK)], MASKED)
                s_ref[g, here, lanes_of(h, BLK)] = masked
                tops.append(fold8(masked, jnp.max))
        return jnp.maximum(top, jnp.concatenate(tops, 1))

    top = lax.fori_loop(0, count, scores, jnp.full((8, groups * lanes), -3e38, F32))
    top = jnp.max(top, 0, keepdims=True)
    acc_ref[...] = jnp.zeros_like(acc_ref)

    def mix(c, total):
        at, _ = key_span(idk_ref, ident_q, start, c, SPAN, window)
        here = pl.ds(pl.multiple_of(c * SPAN * BLK, BLK), SPAN * BLK)
        sums = []
        for g in range(groups):
            e = jnp.exp2(s_ref[g, here, :] - top[:, lanes_of(g, lanes)])
            sums.append(fold8(e, jnp.sum))
            acc_ref[g] += dot_tn(v_ref[at, lanes_of(g)], e.astype(BF))
        return total + jnp.concatenate(sums, 1)

    total = lax.fori_loop(0, count, mix, jnp.zeros((8, groups * lanes), F32))
    total = jnp.sum(total, 0, keepdims=True)
    lse = top + jnp.log(total) * LOG2E
    inverse = 1.0 / total
    for g in range(groups):
        lse_ref[g] = lse[:, lanes_of(g, lanes)]
        acc = acc_ref[g] * inverse[:, lanes_of(g, lanes)]
        out = jnp.concatenate(
            [acc[64 * h : 64 * h + 64, lanes_of(h, BLK)] for h in range(GROUP)], 0
        ).T
        o_ref[:, lanes_of(g)] = out
        low_ref[:, lanes_of(g)] = out.astype(BF)


def stat_spec(groups, base=0):
    return pl.BlockSpec((groups, None, 1, GROUP * BLK), lambda i: (0, i + base, 0, 0))


def query_rows(first, width):
    return pl.BlockSpec(
        (pl.Element(BLK), pl.Element(width)), lambda i: (pl.multiple_of(first + BLK * i, BLK), 0)
    )


def forward_call(bounds, q_win, k_win, v_win, idk, idq, first, own, base, count, earlier=()):
    win, width = k_win.shape
    groups, blocks = width // 256, own // BLK
    row = pl.BlockSpec((BLK, width), lambda i: (i + base, 0))
    steps = -(-win // (SPAN * BLK))
    return pl.pallas_call(
        functools.partial(forward_kernel, first=first, base=base),
        grid=(count,),
        in_specs=[SMEM, query_rows(first + base * BLK, width)]
        + [whole((win, width))] * 2
        + [whole(idk.shape), whole(idq.shape)]
        + [ANY] * len(earlier),
        out_specs=[row, row, stat_spec(groups, base)],
        input_output_aliases={6 + n: n for n in range(len(earlier))},
        out_shape=[
            jax.ShapeDtypeStruct((own, width), F32),
            jax.ShapeDtypeStruct((own, width), BF),
            jax.ShapeDtypeStruct((groups, blocks, 1, GROUP * BLK), F32),
        ],
        scratch_shapes=[
            pltpu.VMEM((groups, steps * SPAN * BLK, GROUP * BLK), F32),
            pltpu.VMEM((groups, 256, GROUP * BLK), F32),
            pltpu.VMEM((groups, GROUP * BLK, 256), BF),
        ],
        compiler_params=params(56),
        cost_estimate=cost(4 * count),
        name="attention_forward",
    )(bounds, q_win, k_win, v_win, idk, idq, *earlier)


def score_gradients(s, dp, lse, delta, seen):
    low_p, low_ds = [], []
    for h in range(GROUP):
        at = lanes_of(h, BLK)
        p = jnp.exp2(jnp.where(seen, s[:, at] * LOG2E - lse[:, at], MASKED))
        low_p.append(p.astype(BF))
        low_ds.append((p * (dp[:, at] - delta[:, at])).astype(BF))
    return jnp.concatenate(low_p, 1), jnp.concatenate(low_ds, 1)


def backward_own_kernel(
    bound_ref, q_ref, do_ref, k_ref, v_ref, idk_ref, idq_ref, lse_ref, delta_ref,
    dq_ref, dk_ref, dv_ref, acc_ref, q4_ref, do4_ref, *, first,
):
    i = pl.program_id(0)
    groups = k_ref.shape[1] // 256
    own = dk_ref.shape[0]

    @pl.when(i == 0)
    def _():
        dk_ref[...] = jnp.zeros_like(dk_ref)
        dv_ref[...] = jnp.zeros_like(dv_ref)

    for g in range(groups):
        q4_ref[g] = head_stack(q_ref[:, lanes_of(g)], True, jnp.asarray(0.125, BF))
        do4_ref[g] = head_stack(do_ref[:, lanes_of(g)], False)
    ident_q = idq_ref[pl.ds(first // BLK + i, 1), :]

    def attend(at, seen, inside):
        for g in range(groups):
            keys = k_ref[at, lanes_of(g)]
            s = dot_nt(keys, q4_ref[g])
            dp = dot_nt(v_ref[at, lanes_of(g)], do4_ref[g])
            low_p, low_ds = score_gradients(s, dp, lse_ref[g], delta_ref[g], seen)
            if inside:
                acc_ref[g] = dot_tn(keys, low_ds)
                dk_ref[:, lanes_of(g)] += dot(low_ds, q4_ref[g])
                dv_ref[:, lanes_of(g)] += dot(low_p, do4_ref[g])
            else:
                acc_ref[g] += dot_tn(keys, low_ds)

    attend(slice(first, first + own), idk_ref[first : first + own, :] == ident_q, True)
    for start, count, end in (
        (bound_ref[i, 2], bound_ref[i, 3], first // BLK),
        ((first + own) // BLK, bound_ref[i, 4], k_ref.shape[0] // BLK),
    ):

        def step(c, _):
            attend(*key_span(idk_ref, ident_q, start, c, SPAN_SIDE, end), False)
            return 0

        lax.fori_loop(0, count, step, 0)
    for g in range(groups):
        acc = acc_ref[g]
        parts = [acc[32 * h : 32 * h + 32, lanes_of(h, BLK)] for h in range(GROUP)]
        parts += [acc[128 + 32 * h : 160 + 32 * h, lanes_of(h, BLK)] for h in range(GROUP)]
        dq_ref[:, lanes_of(g)] = (jnp.concatenate(parts, 0) * 0.125).T


def backward_own_call(bounds, q_win, do_own, k_win, v_win, idk, idq, lse, delta, first, own):
    win, width = k_win.shape
    groups = width // 256
    row = pl.BlockSpec((BLK, width), lambda i: (i, 0))
    return pl.pallas_call(
        functools.partial(backward_own_kernel, first=first),
        grid=(own // BLK,),
        in_specs=[SMEM, query_rows(first, width), row]
        + [whole((win, width))] * 2
        + [whole(idk.shape), whole(idq.shape), stat_spec(groups), stat_spec(groups)],
        out_specs=[row] + [whole((own, width))] * 2,
        out_shape=[jax.ShapeDtypeStruct((own, width), F32)] * 3,
        scratch_shapes=[pltpu.VMEM((groups, 256, GROUP * BLK), F32)]
        + [pltpu.VMEM((groups, GROUP * BLK, 256), BF)] * 2,
        compiler_params=params(24),
        cost_estimate=cost(20),
        name="attention_backward_own",
    )(bounds, q_win, do_own, k_win, v_win, idk, idq, lse, delta)


def backward_halo_kernel(
    bound_ref, q_ref, far_l, near_l, near_r, far_r, k_ref, v_ref, idk_ref, idq_ref, dk_in, dv_in,
    dk_ref, dv_ref, q4_ref, do_all, do4_ref, stat_ref, *, first,
):
    groups = k_ref.shape[1] // 256
    own, reach = k_ref.shape[0], far_l.shape[0] - STAT_PAD
    blocks = own // BLK
    side = first // BLK
    step_id = pl.program_id(0)
    j = jnp.where(step_id < side, step_id, step_id + blocks)
    lanes = GROUP * BLK

    def stats(ref, row, slot):
        parts = ref[row : row + 2 * STAT_ROWS, :].astype(F32)
        sums = parts[0:4] + parts[4:8] + parts[8:12]
        for g in range(groups):
            for n in range(2):
                stat_ref[n, g, slot : slot + 1, :] = jnp.concatenate(
                    [sums[2 * n : 2 * n + 1, lanes_of(g)], sums[2 * n + 1 : 2 * n + 2, lanes_of(g)]],
                    1,
                )

    @pl.when(step_id == 0)
    def _():
        dk_ref[...] = dk_in[...]
        dv_ref[...] = dv_in[...]
        blank = jnp.zeros((BLK - reach, do_all.shape[1]), BF)
        do_all[0 : BLK - reach, :] = blank
        do_all[BLK - reach : BLK, :] = far_l[:reach, :]
        do_all[BLK : BLK + own, :] = near_l[:own, :]
        do_all[BLK + own : BLK + 2 * own, :] = near_r[:own, :]
        do_all[BLK + 2 * own : BLK + 2 * own + reach, :] = far_r[:reach, :]
        do_all[BLK + 2 * own + reach :, :] = blank
        stats(far_l, reach, 0)
        for i in range(blocks):
            stats(near_l, own + 2 * STAT_ROWS * i, 1 + i)
            stats(near_r, own + 2 * STAT_ROWS * i, 1 + blocks + i)
        stats(far_r, reach, 1 + 2 * blocks)

    start, count = bound_ref[j, 0], bound_ref[j, 1]

    @pl.when(count > 0)
    def _():
        here = pl.ds(pl.multiple_of(step_id * BLK, BLK), BLK)
        for g in range(groups):
            q4_ref[g] = head_stack(q_ref[:, lanes_of(g)], True, jnp.asarray(0.125, BF))
            do4_ref[g] = head_stack(do_all[here, lanes_of(g)], False)
        ident_q = idq_ref[pl.ds(j, 1), :]

        def step(c, _):
            at, seen = key_span(idk_ref, ident_q, start, c, SPAN_BACK, blocks)
            for g in range(groups):
                s = dot_nt(k_ref[at, lanes_of(g)], q4_ref[g])
                dp = dot_nt(v_ref[at, lanes_of(g)], do4_ref[g])
                lse = stat_ref[0, g, pl.ds(step_id, 1), :]
                delta = stat_ref[1, g, pl.ds(step_id, 1), :]
                low_p, low_ds = score_gradients(s, dp, lse, delta, seen)
                dk_ref[at, lanes_of(g)] += dot(low_ds, q4_ref[g])
                dv_ref[at, lanes_of(g)] += dot(low_p, do4_ref[g])
            return 0

        lax.fori_loop(0, count, step, 0)


def backward_halo_call(bounds, q_win, pieces, k_win, v_win, idk, idq, dk, dv, first):
    own, width = dk.shape
    groups = width // 256
    side, blocks = first // BLK, own // BLK
    inside = lambda w: pl.BlockSpec(
        (pl.Element(own), pl.Element(w)), lambda i: (pl.multiple_of(first + 0 * i, BLK), 0)
    )
    outside = pl.BlockSpec((BLK, width), lambda i: (jnp.where(i < side, i, i + blocks), 0))
    return pl.pallas_call(
        functools.partial(backward_halo_kernel, first=first),
        grid=(2 * side,),
        in_specs=[SMEM, outside]
        + [whole(p.shape) for p in pieces]
        + [inside(width)] * 2
        + [inside(idk.shape[1]), whole(idq.shape)]
        + [whole((own, width))] * 2,
        out_specs=[whole((own, width))] * 2,
        out_shape=[jax.ShapeDtypeStruct((own, width), F32)] * 2,
        scratch_shapes=[
            pltpu.VMEM((groups, GROUP * BLK, 256), BF),
            pltpu.VMEM((2 * first, width), BF),
            pltpu.VMEM((groups, GROUP * BLK, 256), BF),
            pltpu.VMEM((2, groups, 16, GROUP * BLK), F32),
        ],
        compiler_params=params(20),
        cost_estimate=cost(11),
        name="attention_backward_halo",
    )(bounds, q_win, *pieces, k_win, v_win, idk, idq, dk, dv)


def norm_parts(x):
    centred = x - jnp.mean(x, -1, keepdims=True)
    inverse = lax.rsqrt(jnp.mean(centred * centred, -1, keepdims=True) + EPS)
    return centred * inverse, inverse


def norm_back(grad, xhat, inverse, gain):
    scaled = grad * gain
    return inverse * (
        scaled
        - jnp.mean(scaled, -1, keepdims=True)
        - xhat * jnp.mean(scaled * xhat, -1, keepdims=True)
    )


def columns_sum(x):
    return jnp.sum(x, 0, keepdims=True)


def chip_order(ab, core):
    return jnp.where(core == 0, ab, ab % 2 * 2 + ab // 2)


def slices_out(place, source, keep, away, lead, sem, slices, rows):
    for n in range(slices):
        rel = place ^ n
        for target, odd in ((keep, 0), (away, 1)):
            core = place % 2 ^ odd

            @pl.when(rel % 2 == odd)
            def _():
                pltpu.make_async_copy(
                    source.at[n * rows : (n + 1) * rows, :],
                    target.at[chip_order(rel // 2, core), pl.ds(lead, rows), :],
                    sem.at[n],
                ).start()


def gathered(place, refs):
    for far in range(2):
        for n in range(4):
            rel = 2 * chip_order(jnp.int32(n), place % 2 ^ far) + far
            yield refs[4 * far + n], place ^ rel


def slices_wait(source, keep, sem, slices, rows):
    for n in range(slices):
        pltpu.make_async_copy(
            source.at[n * rows : (n + 1) * rows, :], keep.at[0, 0:rows, :], sem.at[n]
        ).wait()


def one_quarter(q, w_all, norm_ref, dy_ref, bu_ref, dbu_ref, out_acc, dn_acc, g_all, fresh):
    own, width = norm_ref.shape
    tile = w_all.shape[1] - width
    for t in range((w_all.shape[1] - width) // tile):
        cols = slice(tile * t, tile * t + tile)
        down = slice(width + tile * t, width + tile * t + tile)
        norm, dy = norm_ref[...], dy_ref[...]
        up_w = w_all[q, :width, cols]
        down_w = w_all[q, down, :]
        pre = dot(norm, up_w) + bu_ref[pl.ds(q, 1), cols]
        cdf = 0.5 * (1.0 + lax.erf(pre * np.float32(0.7071067811865476)))
        density = jnp.exp(-0.5 * pre * pre) * np.float32(0.3989422804014327)
        act = (pre * cdf).astype(BF)
        d_pre = (dot_nt(dy, down_w) * (cdf + pre * density)).astype(BF)
        dbu_ref[pl.ds(q, 1), cols] = columns_sum(d_pre.astype(F32))
        if fresh and t == 0:
            out_acc[...] = dot(act, down_w)
            dn_acc[...] = dot_nt(d_pre, up_w)
        else:
            out_acc[...] += dot(act, down_w)
            dn_acc[...] += dot_nt(d_pre, up_w)
        g_all[q, :width, cols] = dot_tn(norm, d_pre).astype(BF)
        g_all[q, down, :] = dot_tn(act, dy).astype(BF)


def middle_own_kernel(
    place_ref, x_ref, low_ref, wo_ref, vec_ref, dy_ref, bu_ref, up_ref, down_ref,
    hid_ref, norm_ref, out_ref, dn_ref, dbu_ref, keep_ref, send_ref, w_all, g_all, w_sem, g_sem,
    *, slices,
):
    width = x_ref.shape[1]
    rows = w_all.shape[1] // slices
    copies = [
        pltpu.make_async_copy(up_ref, w_all.at[0, :width, :], w_sem.at[0]),
        pltpu.make_async_copy(down_ref, w_all.at[0, width:, :], w_sem.at[1]),
    ]
    for copy in copies:
        copy.start()
    hidden_in = x_ref[...].astype(F32) + dot(low_ref[...], wo_ref[...]) + vec_ref[B_OUT]
    hid_ref[...] = hidden_in
    norm_ref[...] = layer_norm_low(hidden_in, vec_ref[LN2_GAIN], vec_ref[LN2_SHIFT])
    for copy in copies:
        copy.wait()
    one_quarter(0, w_all, norm_ref, dy_ref, bu_ref, dbu_ref, out_ref, dn_ref, g_all, True)
    slices_out(place_ref[0], g_all.at[0], keep_ref, send_ref, 0, g_sem, slices, rows)
    slices_wait(g_all.at[0], keep_ref, g_sem, slices, rows)


def middle_own_call(place, x, low, w_out, vectors, dy, b_up, w_up, w_down, slices):
    own, width = x.shape
    hidden = b_up.shape[1]
    rows = width + hidden
    vmem = pl.BlockSpec(memory_space=pltpu.VMEM)
    sds = jax.ShapeDtypeStruct
    return pl.pallas_call(
        functools.partial(middle_own_kernel, slices=slices),
        in_specs=[SMEM] + [vmem] * 6 + [ANY] * 2,
        out_specs=[vmem] * 5 + [ANY] * 2,
        out_shape=[
            sds((own, width), F32),
            sds((own, width), BF),
            sds((own, width), F32),
            sds((own, width), F32),
            sds((1, hidden), F32),
        ]
        + [sds((slices // 2, rows // slices, width), BF)] * 2,
        scratch_shapes=[
            pltpu.VMEM((1, rows, width), BF),
            pltpu.VMEM((1, rows, width), BF),
            pltpu.SemaphoreType.DMA((2,)),
            pltpu.SemaphoreType.DMA((slices,)),
        ],
        compiler_params=params(56),
        cost_estimate=cost(12),
        name="middle_own",
    )(place, x, low, w_out, vectors, dy, b_up, w_up, w_down)


def middle_kernel(
    place_ref, vec_ref, bu_ref, lse_ref, norm_in, dy_in, out_in, dn_in, hid_in, low_in, mixed_in,
    wo_in, *refs, slices,
):
    piece_refs = refs[:slices]
    (
        act_out, dh_out, dheads_ref, head_ref, tail_ref, delta_ref, small_ref, dbu_ref, keep_ref,
        send_ref,
        w_all, g_all, go_all, norm_ref, dy_ref, out_acc, dn_acc, hid_ref, low_ref, mixed_ref,
        wo_ref, act_ref, dh_ref, w_sem, g_sem, in_sem, out_sem,
    ) = refs[slices:]
    place = place_ref[0]
    own, width = norm_ref.shape
    quarters = w_all.shape[0]
    rows = w_all.shape[1] // slices

    def fetches(q):
        return [
            pltpu.make_async_copy(
                ref.at[q],
                w_all.at[q, pl.ds(pl.multiple_of(source * rows, rows), rows), :],
                w_sem.at[q, n],
            )
            for n, (ref, source) in enumerate(gathered(place, piece_refs))
        ]

    inputs = [
        pltpu.make_async_copy(source, target, in_sem.at[n])
        for n, (source, target) in enumerate(
            (
                (norm_in, norm_ref), (dy_in, dy_ref), (out_in, out_acc), (dn_in, dn_acc),
                (hid_in, hid_ref), (low_in, low_ref), (mixed_in, mixed_ref), (wo_in, wo_ref),
            )
        )
    ]
    for copy in inputs[:2] + fetches(0) + inputs[2:4]:
        copy.start()
    for q in range(1, quarters):
        for copy in fetches(q):
            copy.start()
    for copy in inputs[4:]:
        copy.start()
    for copy in inputs[:2]:
        copy.wait()

    def quarter(q, _):
        for copy in fetches(q):
            copy.wait()

        @pl.when(q == 0)
        def _():
            for copy in inputs[2:4]:
                copy.wait()

        one_quarter(q, w_all, norm_ref, dy_ref, bu_ref, dbu_ref, out_acc, dn_acc, g_all, False)
        slices_out(
            place, g_all.at[q], keep_ref, send_ref, pl.multiple_of(q * rows, rows),
            g_sem.at[q], slices, rows,
        )
        return 0

    lax.fori_loop(0, quarters, quarter, 0)

    for copy in inputs[4:]:
        copy.wait()
    hidden_in = hid_ref[...]
    xhat, inverse = norm_parts(hidden_in)
    dn = dn_acc[...]
    dy = dy_ref[...].astype(F32)
    d_hidden = dy + norm_back(dn, xhat, inverse, vec_ref[LN2_GAIN])
    dh_ref[...] = d_hidden
    d_att = d_hidden.astype(BF)
    d_heads = dot_nt(d_att, wo_ref[...]).astype(BF)
    dheads_ref[:own, :] = d_heads
    go_all[...] = dot_tn(low_ref[...], d_att).astype(BF)
    few = width // slices
    base = quarters * rows
    slices_out(place, go_all, keep_ref, send_ref, base, g_sem.at[quarters], slices, few)
    act_ref[...] = (hidden_in + out_acc[...] + vec_ref[B_DOWN]).astype(BF)
    outputs = [
        pltpu.make_async_copy(source, target, out_sem.at[n])
        for n, (source, target) in enumerate(
            (
                (act_ref, act_out), (dh_ref, dh_out),
            )
        )
    ]
    for copy in outputs:
        copy.start()
    small_ref[0:1, :] = columns_sum(dn * xhat)
    small_ref[1:2, :] = columns_sum(dn)
    small_ref[2:3, :] = columns_sum(dy)
    small_ref[3:4, :] = columns_sum(d_att.astype(F32))
    spread = d_heads.astype(F32) * mixed_ref[...]
    pick = lax.broadcasted_iota(jnp.int32, (8, 256), 0)
    pick = (pick == lax.broadcasted_iota(jnp.int32, (8, 256), 1) // 64).astype(F32)
    for g in range(width // 256):
        for i in range(own // BLK):
            block = spread[BLK * i : BLK * i + BLK, 256 * g : 256 * g + 256]
            sums = lax.dot_general(
                pick, block, (((1,), (1,)), ((), ())),
                preferred_element_type=F32, precision=lax.Precision.HIGHEST,
            )
            delta = jnp.concatenate([sums[h : h + 1, :] for h in range(GROUP)], 1)
            delta_ref[g, i] = delta
            lse = lse_ref[g, i]
            left = jnp.concatenate(
                [lse[:, :256], lse[:, 256:], delta[:, :256], delta[:, 256:]], 0
            )
            parts = []
            for _ in range(3):
                parts.append(left.astype(BF))
                left = left - parts[-1].astype(F32)
            parts = jnp.concatenate(parts, 0)
            at = slice(256 * g, 256 * g + 256)
            lo = own + 2 * STAT_ROWS * i
            dheads_ref[lo : lo + 2 * STAT_ROWS, at] = parts
            for target, row in ((head_ref, 0), (tail_ref, own // BLK - 1)):
                if i == row:
                    target[REACH : REACH + 2 * STAT_ROWS, at] = parts
    blank = jnp.zeros((STAT_PAD - 2 * STAT_ROWS, width), BF)
    head_ref[REACH + 2 * STAT_ROWS :, :] = blank
    tail_ref[REACH + 2 * STAT_ROWS :, :] = blank
    head_ref[:REACH, :] = d_heads[:REACH, :]
    tail_ref[:REACH, :] = d_heads[own - REACH :, :]
    for q in range(quarters):
        slices_wait(g_all.at[q], keep_ref, g_sem.at[q], slices, rows)
    slices_wait(go_all, keep_ref, g_sem.at[quarters], slices, few)
    for copy in outputs:
        copy.wait()


def middle_call(
    place, hidden_in, norm, out, dn, low, mixed, w_out, vectors, dy, b_up, lse, pieces, slices,
):
    own, width = norm.shape
    quarters, hidden = b_up.shape
    rows = width + hidden
    vmem = pl.BlockSpec(memory_space=pltpu.VMEM)
    sds = jax.ShapeDtypeStruct
    grads = sds((slices // 2, (quarters * rows + width) // slices, width), BF)
    return pl.pallas_call(
        functools.partial(middle_kernel, slices=slices),
        in_specs=[SMEM] + [vmem] * 3 + [ANY] * (8 + len(pieces)),
        out_specs=[ANY] * 2 + [vmem] * 6 + [ANY] * 2,
        out_shape=[
            sds((own, width), BF),
            sds((own, width), F32),
            sds((own + own // BLK * 2 * STAT_ROWS, width), BF),
            sds((REACH + STAT_PAD, width), BF),
            sds((REACH + STAT_PAD, width), BF),
            sds((width // 256, own // BLK, 1, GROUP * BLK), F32),
            sds((4, width), F32),
            sds((quarters, hidden), F32),
            grads,
            grads,
        ],
        scratch_shapes=[
            pltpu.VMEM((quarters, rows, width), BF),
            pltpu.VMEM((quarters, rows, width), BF),
            pltpu.VMEM((width, width), BF),
            pltpu.VMEM((own, width), BF),
            pltpu.VMEM((own, width), BF),
            pltpu.VMEM((own, width), F32),
            pltpu.VMEM((own, width), F32),
            pltpu.VMEM((own, width), F32),
            pltpu.VMEM((own, width), BF),
            pltpu.VMEM((own, width), F32),
            pltpu.VMEM((width, width), BF),
            pltpu.VMEM((own, width), BF),
            pltpu.VMEM((own, width), F32),
            pltpu.SemaphoreType.DMA((quarters, slices)),
            pltpu.SemaphoreType.DMA((quarters + 1, slices)),
            pltpu.SemaphoreType.DMA((10,)),
            pltpu.SemaphoreType.DMA((4,)),
        ],
        compiler_params=params(44),
        cost_estimate=cost(20),
        name="middle",
    )(
        place, vectors, b_up, lse, norm, dy, out, dn, hidden_in, low, mixed, w_out, *pieces,
    )


def turn_back_kernel(
    place_ref, x_ref, vec_ref, dq_ref, dk_ref, dv_ref, q_ref, k_ref, hot_ref, table_ref, grid_ref,
    back_ref, d_ref, db_ref, freq_ref, keep_ref, send_ref, norm_ref, g_all, sem, *, slices,
):
    width = x_ref.shape[1]
    group = pl.program_id(0)

    @pl.when(group == 0)
    def _():
        norm_ref[...] = layer_norm_low(
            x_ref[...].astype(F32), vec_ref[LN1_GAIN], vec_ref[LN1_SHIFT]
        )

    c, s = cos_sin(hot_ref[...], table_ref[...])
    norm = norm_ref[...]

    def gradient(n, low):
        d_ref[n] = low
        db_ref[n : n + 1, :] = columns_sum(low.astype(F32))
        at = pl.ds(pl.multiple_of(n * width + group * 256, 256), 256)
        g_all[:, at] = dot_tn(norm, low).astype(BF)

    d_angle = 0.0
    for n, (grad, turned_ref) in enumerate(((dq_ref, q_ref), (dk_ref, k_ref))):
        g1, g2 = grad[:, :128], grad[:, 128:]
        d_angle = d_angle + (g2 * turned_ref[:, :128] - g1 * turned_ref[:, 128:])
        back = jnp.concatenate([g1 * c + g2 * s, g2 * c - g1 * s], 1).astype(BF)
        gradient(n, dot(back, back_ref[...]).astype(BF))
    freq_ref[...] = lax.dot_general(
        grid_ref[...], d_angle, (((1,), (0,)), ((), ())),
        preferred_element_type=F32, precision=lax.Precision.HIGHEST,
    )
    gradient(2, dv_ref[...].astype(BF))

    @pl.when(group == width // 256 - 1)
    def _():
        slices_out(place_ref[0], g_all, keep_ref, send_ref, 0, sem, slices, width // slices)
        slices_wait(g_all, keep_ref, sem, slices, width // slices)


def turn_back_call(
    place, x, vectors, dq, dk, dv, q_exact, k_exact, onehot, table, grid8, back, first, slices
):
    rows, width = dk.shape
    sds = jax.ShapeDtypeStruct
    part = pl.BlockSpec((rows, 256), lambda g: (0, g))
    hot = pl.BlockSpec(
        (pl.Element(rows), pl.Element(onehot.shape[1])),
        lambda g: (pl.multiple_of(first + 0 * g, BLK), 0),
    )
    return pl.pallas_call(
        functools.partial(turn_back_kernel, slices=slices),
        grid=(width // 256,),
        in_specs=[SMEM, whole(x.shape), whole(vectors.shape)]
        + [part] * 5
        + [
            hot,
            pl.BlockSpec((table.shape[0], 512), lambda g: (0, g)),
            whole(grid8.shape),
            whole(back.shape),
        ],
        out_specs=[
            pl.BlockSpec((3, rows, 256), lambda g: (0, 0, g)),
            pl.BlockSpec((3, 256), lambda g: (0, g)),
            pl.BlockSpec((8, 128), lambda g: (0, g)),
        ]
        + [ANY] * 2,
        out_shape=[
            sds((3, rows, width), BF),
            sds((3, width), F32),
            sds((8, width // 2), F32),
        ]
        + [sds((slices // 2, width // slices, 3 * width), BF)] * 2,
        scratch_shapes=[
            pltpu.VMEM((rows, width), BF),
            pltpu.VMEM((width, 3 * width), BF),
            pltpu.SemaphoreType.DMA((slices,)),
        ],
        compiler_params=params(16),
        cost_estimate=cost(9),
        name="turn_back",
    )(place, x, vectors, dq, dk, dv, q_exact, k_exact, onehot, table, grid8, back)


def input_grad_kernel(
    place_ref, x_ref, vec_ref, d_ref, w_ref, dh_ref, db_ref, mid_ref, freq_ref, up0_ref, up_ref,
    out_ref, small_ref,
):
    width = x_ref.shape[1]
    d_norm = sum(dot_nt(d_ref[n], w_ref[:, lanes_of(n, width)]) for n in range(3))
    xhat, inverse = norm_parts(x_ref[...].astype(F32))
    out_ref[...] = dh_ref[...] + norm_back(d_norm, xhat, inverse, vec_ref[LN1_GAIN])
    row = 0
    for vector in (
        columns_sum(d_norm * xhat), columns_sum(d_norm), *(db_ref[n : n + 1, :] for n in range(3)),
        mid_ref[3:4, :], freq_ref[0:1, :], freq_ref[1:2, :], *(mid_ref[n : n + 1, :] for n in range(3)),
    ):
        for n in range(vector.shape[1] // 128):
            small_ref[row : row + 1, :] = vector[:, lanes_of(n, 128)]
            row += 1
    depth = 1 + up_ref.shape[0]
    hidden = up0_ref.shape[1] // 128
    for k in range(depth):
        quarter = (place_ref[1] - k + depth) % depth
        vector = up_ref[k - 1 : k, :] if k else up0_ref[...]
        for n in range(hidden):
            small_ref[pl.ds(row + quarter * hidden + n, 1), :] = vector[:, lanes_of(n, 128)]


def input_grad_call(place, x, vectors, d_qkv, weight, d_hidden, db_qkv, small_mid, freqs, up0, up):
    rows, width = x.shape
    short = 9 * width + freqs.shape[1] * 2 + up0.size * (1 + up.shape[0])
    return pl.pallas_call(
        input_grad_kernel,
        in_specs=[SMEM] + [pl.BlockSpec(memory_space=pltpu.VMEM)] * 10,
        out_shape=[
            jax.ShapeDtypeStruct((rows, width), F32),
            jax.ShapeDtypeStruct((short // 128, 128), F32),
        ],
        compiler_params=params(20),
        cost_estimate=cost(7),
        name="input_grad",
    )(place, x, vectors, d_qkv, weight, d_hidden, db_qkv, small_mid, freqs, up0, up)


def assemble_kernel(place_ref, *refs, split, outs, skip):
    out_refs, (held, sem) = refs[-2 - outs : -2], refs[-2:]
    pairs = refs[:4]
    piece_refs = [pairs[n // 2].at[n % 2] for n in range(8)]
    place, depth = place_ref[0], place_ref[1]
    slot = pl.program_id(0)

    def copy(ref, target):
        return pltpu.make_async_copy(ref, held.at[target], sem.at[target])

    @pl.when(slot == 0)
    def _():
        for ref, source in gathered(place, piece_refs):
            copy(ref, source).start()

    copy(piece_refs[0], slot).wait()
    rows = held.shape[-2]
    total_ref = None
    if skip is not None:
        out_refs, total_ref = out_refs[:-1], out_refs[-1]
    out_refs, squares = out_refs[:-1], out_refs[-1]

    @pl.when(slot == 0)
    def _():
        squares[...] = jnp.zeros_like(squares)

    def add_squares(block):
        total = fold8(block * block, jnp.sum)
        squares[...] += sum(total[:, lanes_of(n, 128)] for n in range(block.shape[1] // 128))

    if split:
        for n in range(split):
            block = held[slot, (depth - n + split) % split].astype(F32)
            add_squares(block)
            lo = 0
            for ref in out_refs:
                ref[n * rows : n * rows + rows, :] = block[:, lo : lo + ref.shape[1]]
                lo += ref.shape[1]
    else:
        block = held[slot].astype(F32)
        add_squares(block)
        each = held.shape[0] // len(out_refs)
        for n, ref in enumerate(out_refs):

            @pl.when(slot // each == n)
            def _():
                ref[...] = block
    if skip is not None:
        small_ref = refs[4]

        @pl.when(slot == held.shape[0] - 1)
        def _():
            short = small_ref[...]
            row = lax.broadcasted_iota(jnp.int32, short.shape, 0)
            mine = (row >= skip[0]) & (row < skip[1])
            parts = row >= short.shape[0] - 8
            others = jnp.where(mine, 0.0, jnp.where(parts, short, short * short))
            turned = jnp.where(mine, short * short, 0.0)
            total_ref[0:1, :] = jnp.full((1, 128), jnp.sum(turned))
            total_ref[1:2, :] = jnp.full((1, 128), jnp.sum(others) + jnp.sum(squares[...]))


def assemble_call(place, arrays, shapes, split, small=None, skip=None):
    pieces = 8
    rows = arrays[0].shape[-2] * max(split, 1)
    each = pieces if split else pieces // len(shapes)

    def spec(n, shape):
        lead = 0 if split else n * each
        return pl.BlockSpec((rows, shape[1]), lambda i: (jnp.clip(i - lead, 0, each - 1), 0))

    specs = [spec(n, shape) for n, shape in enumerate(shapes)] + [whole((8, 128))]
    shapes = shapes + [(8, 128)]
    given = []
    if small is not None:
        given, specs, shapes = [small], specs + [whole((2, 128))], shapes + [(2, 128)]
    return pl.pallas_call(
        functools.partial(assemble_kernel, split=split, outs=len(shapes), skip=skip),
        grid=(pieces,),
        in_specs=[SMEM] + [ANY] * len(arrays) + [whole(x.shape) for x in given],
        out_specs=specs,
        out_shape=[jax.ShapeDtypeStruct(s, F32) for s in shapes],
        scratch_shapes=[
            pltpu.VMEM((pieces,) + arrays[0].shape[1:], BF),
            pltpu.SemaphoreType.DMA((pieces,)),
        ],
        compiler_params=params(16),
        cost_estimate=cost(6),
        name="assemble",
    )(place, *arrays, *given)


def send(x, axis, pairs):
    return lax.ppermute(x, axis, pairs)


def plane_gather(piece):
    pair = jnp.stack([piece, send(piece, PLANE, FIRST)])
    return pair, send(pair, PLANE, SECOND)


def core_gather(pair, last):
    return [pair, last, send(pair, "c", SWAP), send(last, "c", SWAP)]


def wide_sum(x, extra):
    return lax.psum(x, "e") if extra > 1 else x


def sum_low(*terms):
    return functools.reduce(lambda x, y: x + y, [t.astype(F32) for t in terms])


def after(x, *others):
    return lax.optimization_barrier((x, others))[0]


def ring(size, step):
    return [(i, (i + step) % size) for i in range(size)]


def add_from(vector, axis, reach=0, size=2):
    return vector + send(vector, axis, [(i, i ^ (reach or 1)) for i in range(size)])


def on_device(
    tokens,
    segment,
    padding,
    coords,
    ln1_gain,
    ln1_shift,
    query_key_value_weight,
    b_qkv,
    output_weight,
    b_out,
    rope_freqs,
    ln2_gain,
    ln2_shift,
    w_up,
    b_up,
    w_down,
    b_down,
    cotangent,
    *,
    extra,
    depth,
):
    tokens, cotangent = tokens[0], cotangent[0]
    own, width = tokens.shape
    length = own * depth
    heads = rope_freqs.shape[1]
    half = width // heads // 2
    groups = heads // GROUP
    slices = 8
    outer = BLK
    side = own + outer
    win = own + 2 * side
    blocks = own // BLK
    z = lax.axis_index("n")
    plane = lax.axis_index("a") * 4 + lax.axis_index("b") * 2 + lax.axis_index("c")
    place = jnp.stack([plane, z]).astype(jnp.int32)
    up = [(i, i + 1) for i in range(depth - 1)]
    down = [(i + 1, i) for i in range(depth - 1)]
    up2 = [(i, i + 2) for i in range(depth - 2)]
    down2 = [(i + 2, i) for i in range(depth - 2)]

    def around(x, head, tail):
        before2 = send(tail, "n", up2)
        before = send(x, "n", up)
        after_ = send(x, "n", down)
        after2 = send(head, "n", down2)
        return [before2, before, after_, after2]

    position = jnp.arange(length, dtype=jnp.int32)
    ident = jnp.where(padding[0] == 0, segment[0], 1000 + position)
    ident = jnp.concatenate(
        [jnp.full((side,), -1, jnp.int32), ident, jnp.full((side,), 1 << 20, jnp.int32)]
    )
    ident_win = lax.dynamic_slice_in_dim(ident, z * own, win, 0)
    near = lax.broadcasted_iota(jnp.int32, (win,), 0)
    ident_win = jnp.where(near < outer - REACH, -1, ident_win)
    ident_win = jnp.where(near >= win - outer + REACH, 1 << 20, ident_win)
    idk = jnp.broadcast_to(ident_win[:, None], (win, BLK))
    idq = ident_win.reshape(win // BLK, BLK)

    lowest, highest = idq[:, 0], idq[:, BLK - 1]

    def bounds(queries, keys):
        before = highest[keys][None, :] < lowest[queries][:, None]
        reached = lowest[keys][None, :] <= highest[queries][:, None]
        return jnp.sum(before, 1), jnp.sum(reached, 1)

    def steps(blocks, span):
        return (jnp.maximum(blocks, 0) + span - 1) // span

    mid = slice(side // BLK, side // BLK + blocks)
    lo, hi = bounds(mid, slice(None))
    bounds_fwd = [
        lo, steps(hi - lo, SPAN), jnp.minimum(lo, mid.start), steps(mid.start - lo, SPAN_SIDE),
        steps(hi - mid.stop, SPAN_SIDE),
    ]
    bounds_fwd = jnp.stack(bounds_fwd, 1).astype(jnp.int32)
    lo, hi = bounds(slice(None), mid)
    bounds_bwd = jnp.stack([lo, steps(hi - lo, SPAN_BACK)], 1).astype(jnp.int32)

    grid = jnp.pad(coords[:, 0], ((0, 0), (side, side)))
    grid_win = lax.dynamic_slice_in_dim(grid, z * own, win, 1)
    grid_own = lax.dynamic_slice_in_dim(grid, z * own + side, own, 1)
    lane = jnp.arange(4 * SIDE)
    picked = jnp.where(lane[None, :] < 2 * SIDE, grid_win[0][:, None], grid_win[1][:, None])
    onehot = (picked == (lane % SIDE)[None, :]).astype(BF)
    table = turn_table(rope_freqs)

    local = np.arange(256)
    order = np.zeros((256, 256), np.float32)
    order[(local % 128) // 32 * 64 + local // 128 * 32 + local % 32, local] = 1.0
    order = jnp.asarray(order, BF)
    qk_bias = b_qkv[: 2 * width].reshape(2 * groups, GROUP, 2, half).swapaxes(1, 2)
    bias_turned = jnp.concatenate([qk_bias.reshape(-1), b_qkv[2 * width :]])

    x_parts = around(tokens, tokens[:REACH], tokens[own - REACH :])
    vectors = jnp.stack([ln1_gain, ln1_shift, b_out, ln2_gain, ln2_shift, b_down])
    rot_q, rot_k, values, q_exact, k_exact, weight_turned = qkv_own_call(
        tokens, onehot, vectors, query_key_value_weight, bias_turned, order, table, side
    )
    rows = (width + w_down.shape[0]) // slices
    eighth = jnp.where(
        plane < width // rows,
        lax.dynamic_slice_in_dim(w_up, jnp.minimum(plane * rows, width - rows), rows, 0),
        lax.dynamic_slice_in_dim(w_down, jnp.maximum(plane * rows - width, 0), rows, 0),
    )
    left, bias_rows = b_up, []
    for _ in range(3):
        bias_rows.append(left.astype(BF))
        left = left - rounded(left)
    bias_rows = jnp.pad(jnp.stack(bias_rows), ((0, 13), (0, 0)))
    eighth = jnp.concatenate([eighth, bias_rows], 0)
    others = [send(eighth, "n", ring(depth, k)) for k in range(1, depth)]
    x_parts, rot_q, idk = lax.optimization_barrier((x_parts, rot_q, idk))
    halo_args = (x_parts, onehot, vectors, weight_turned, bias_turned, table)
    rot_q, rot_k, values = halo_call(*halo_args, (rot_q, rot_k, values), (0, 1, 2), side)
    part = forward_call(bounds_fwd, rot_q, rot_k, values, idk, idq, side, own, 0, blocks // 2)
    others, part = lax.optimization_barrier((others, part))
    up_biases = jnp.concatenate(
        [jnp.sum(x[rows : rows + 3].astype(F32), 0, keepdims=True) for x in others]
    )
    own_w = jnp.stack([x[:rows] for x in others])
    over_1, over_2 = send(own_w, PLANE, FIRST), send(own_w, PLANE, SECOND)
    part, _ = lax.optimization_barrier((part, own_w))
    mixed, mixed_low, lse = forward_call(
        bounds_fwd, rot_q, rot_k, values, idk, idq, side, own, blocks // 2, blocks // 2, part
    )
    hidden_in, norm2, out0, dn0, up_sum0, kept_own, sent_own = middle_own_call(
        place, tokens, mixed_low, output_weight, vectors, cotangent, b_up[None],
        w_up, w_down, slices,
    )
    over_1, over_2, norm2 = lax.optimization_barrier((over_1, over_2, norm2))
    diagonal = send(over_1, PLANE, SECOND)
    near = [own_w, over_1, over_2, diagonal]
    pieces = near + [send(x, "c", SWAP) for x in near]
    grid8 = jnp.pad(grid_own.astype(F32), ((0, 6), (0, 0)))
    far_own = send(after(sent_own, over_1, over_2), "c", SWAP)
    away_own = sum_low(kept_own[1::2], far_own[1::2]).astype(BF)
    got_own = [send(away_own, PLANE, FIRST)]
    norm2, up_biases, bounds_bwd, _ = lax.optimization_barrier(
        (norm2, up_biases, bounds_bwd, away_own)
    )
    (
        activations, d_hidden, d_heads, d_head, d_tail, delta, small_mid, up_sums, kept_mid,
        sent_mid,
    ) = middle_call(
        place, hidden_in, norm2, out0, dn0, mixed_low, mixed, output_weight, vectors, cotangent,
        up_biases, lse, pieces, slices,
    )
    far_mid = send(sent_mid, "c", SWAP)
    do_parts = around(d_heads, d_head, d_tail)

    got_own[0], far_mid = lax.optimization_barrier((got_own[0], far_mid))
    away_own = sum_low(kept_own[2], far_own[2], got_own[0][1]).astype(BF)
    got_own.append(send(away_own, PLANE, SECOND))
    away = sum_low(kept_mid[1::2], far_mid[1::2]).astype(BF)
    got_1 = send(away, PLANE, FIRST)
    dq, dk, dv = backward_own_call(
        bounds_fwd, rot_q, d_heads, rot_k, values, idk, idq, lse, after(delta, away, away_own),
        side, own,
    )
    got_1, got_own[1], dq = lax.optimization_barrier((got_1, got_own[1], dq))
    away = sum_low(kept_mid[2], far_mid[2], got_1[1]).astype(BF)
    got_2 = send(away, PLANE, SECOND)
    do_parts, dq, dk, _ = lax.optimization_barrier((do_parts, dq, dk, away))
    dk, dv = backward_halo_call(
        bounds_bwd, rot_q, do_parts, rot_k, values, idk, idq, dk, dv, side
    )
    got_2, dk = lax.optimization_barrier((got_2, dk))

    def plane_part(lo, hi):
        at = slice(lo, hi)
        total = sum_low(kept_mid[0, at], far_mid[0, at], got_1[0, at], got_2[at])
        return wide_sum(total, extra)

    ff_sent = [plane_part(k * rows - rows, k * rows).astype(BF) for k in range(1, depth)]
    ff_got = [send(x, "n", ring(depth, -1 - k)) for k, x in enumerate(ff_sent)]
    dk = after(dk, ff_sent)

    d_qkv, grad_b_qkv, freqs8, kept_qkv, sent_qkv = turn_back_call(
        place, tokens, vectors, dq, dk, dv, q_exact, k_exact, onehot, table, grid8,
        order.T, side, slices,
    )
    far_qkv = send(sent_qkv, "c", SWAP)
    away = sum_low(kept_qkv[1::2], far_qkv[1::2]).astype(BF)
    got_1_qkv = send(away, PLANE, FIRST)
    input_grad, small_in = input_grad_call(
        place, tokens, vectors, after(d_qkv, away), query_key_value_weight, d_hidden,
        grad_b_qkv, small_mid, freqs8, up_sum0, up_sums,
    )
    got_1_qkv, small_in = lax.optimization_barrier((got_1_qkv, small_in))
    away = sum_low(kept_qkv[2], far_qkv[2], got_1_qkv[1]).astype(BF)
    got_2_qkv = send(away, PLANE, SECOND)
    ff_got, small_in, _ = lax.optimization_barrier((ff_got, small_in, away))
    plane_qkv = wide_sum(sum_low(kept_qkv[0], far_qkv[0], got_1_qkv[0], got_2_qkv), extra)
    ff_total = wide_sum(sum_low(kept_own[0], far_own[0], got_own[0][0], got_own[1]), extra)
    ff_total = ff_total + sum_low(*ff_got)

    sizes = [width, width, 3 * width, width, rope_freqs.size] + [width] * 3 + [b_up.size * depth]
    small = add_from(small_in, "c")

    part = plane_part((depth - 1) * rows, (depth - 1) * rows + width // slices)
    part = jnp.concatenate([plane_qkv, part], 1).astype(BF)
    thin = part.shape[0] // depth
    cut = lambda k: lax.dynamic_slice_in_dim(part, ((z + k) % depth) * thin, thin, 0)
    got = [send(cut(k), "n", ring(depth, k)) for k in range(1, depth)]
    small = add_from(add_from(after(small, part), "b"), "a")
    if extra > 1:
        small = lax.psum(small, "e")
    got, small = lax.optimization_barrier((got, small))
    low = sum_low(cut(0), *got).astype(BF)
    strip = jnp.stack([low] + [send(low, "n", ring(depth, k)) for k in range(1, depth)])
    ff_pair, ff_last = plane_gather(after(ff_total, low).astype(BF))
    pair, last = plane_gather(strip)
    ff_pieces = [after(x, strip) for x in core_gather(ff_pair, ff_last)]
    total_w_up, total_w_down, ff_squares = assemble_call(
        place, ff_pieces, [w_up.shape, w_down.shape], 0
    )
    small = jnp.concatenate([small, ff_squares], 0)
    reach = 1
    while reach < depth:
        small = add_from(small, "n", reach, depth)
        reach *= 2
    last, small = lax.optimization_barrier((last, small))
    turned = sum(sizes[:4]) // 128
    total_w_qkv, total_w_out, _, norms = assemble_call(
        place, core_gather(pair, last), [query_key_value_weight.shape, output_weight.shape], depth,
        small, (turned, turned + sizes[4] // 128),
    )
    small = small[:-8].reshape(-1)
    out, at = [], 0
    for size in sizes:
        out.append(small[at : at + size])
        at += size
    t_gain1, t_shift1, t_b_qkv, t_b_out, t_freqs, t_gain2, t_shift2, t_b_down, t_up = out
    t_freqs = t_freqs.reshape(rope_freqs.shape)
    rot_sq, other_sq = norms[0, 0], norms[1, 0]
    t_b_up = lax.dynamic_slice_in_dim(t_up, z * b_up.shape[0], b_up.shape[0], 0)
    return (
        activations[None],
        input_grad[None],
        t_gain1,
        t_shift1,
        total_w_qkv,
        t_b_qkv,
        total_w_out,
        t_b_out,
        t_freqs,
        t_gain2,
        t_shift2,
        total_w_up,
        t_b_up,
        total_w_down,
        t_b_down,
        rot_sq,
        other_sq,
    )


def solution(mesh):
    wide, depth = mesh.shape["wide"], mesh.shape["narrow"]
    extra = wide // 8
    fine = Mesh(mesh.devices.reshape(extra, 2, 2, 2, depth), ("e", "a", "b", "c", "n"))
    w, n = ("e", "a", "b", "c"), "n"
    return jax.shard_map(
        functools.partial(on_device, extra=extra, depth=depth),
        mesh=fine,
        in_specs=(
            P(w, n, None), P(w, None), P(w, None), P(None, w, None),
            P(), P(), P(), P(), P(), P(), P(), P(), P(),
            P(None, n), P(n), P(n, None), P(), P(w, n, None),
        ),
        out_specs=(
            P(w, n, None), P(w, n, None),
            P(), P(), P(), P(), P(), P(), P(), P(), P(),
            P(None, n), P(n), P(n, None), P(), P(), P(),
        ),
        check_vma=False,
    )
```

profile of v0, /device:TPU:1, one launch (start us, length us, event | category | flops | bytes accessed | tf_op | source)
XLA Modules:
  0.0 307.1 jit_solution(16084753507873069776)
XLA Ops:
  0.7 5.1 %collective-permute-start.4 = (bf16[512,768]{1,0:T(8,128)(2,1)}, bf16[512,768]{1,0:T(8,128)(2,1)}, u32[]{:S(2)}, u32[]{:S(2)}) collective-permute-start(bf16[512,768]{1,0:T(8,128)(2,1)} %bitcast.92), channel_id=1, source_target_pairs={{0,1},{1,2},{2,3},{4,5},{5,6},{6,7},{8,9},{9,10},{10,11},{12,13},{... | collective-permute-start | bytes 2359304 | tf_op jit(solution)/shard_map/ppermute | solution.py:1048
  8.1 4.1 %collective-permute-start.3 = (bf16[64,768]{1,0:T(8,128)(2,1)S(1)}, bf16[64,768]{1,0:T(8,128)(2,1)S(1)}, u32[]{:S(2)}, u32[]{:S(2)}) collective-permute-start(bf16[64,768]{1,0:T(8,128)(2,1)S(1)} %get-tuple-element.324), channel_id=1, source_target_pairs={{0,2},{1,3},{4,6},{5,7},{8,10},{9,11},{12,14},{13,15},{16,18},{17,... | collective-permute-start | bytes 294920 | tf_op jit(solution)/shard_map/ppermute | solution.py:1048
  15.6 2.2 collective-permute-start
  23.2 1.7 fusion.1.hot_ref
  26.2 8.8 %qkv_own.1 = (bf16[1792,768]{1,0:T(8,128)(2,1)}, bf16[1792,768]{1,0:T(8,128)(2,1)}, bf16[1792,768]{1,0:T(8,128)(2,1)}, f32[512,768]{1,0:T(8,128)}, f32[512,768]{1,0:T(8,128)}, /*index=5*/bf16[768,2304]{1,0:T(8,128)(2,1)}) custom-call(bf16[512,768]{1,0:T(8,128)(2,1)} %bitcast.94, bf16[1792,128]{1,0:T(8,128)(2,1)} %fusion.1.hot_ref, f32[6,768]{1,0:T(8,128)} %stack.113.vec_ref, ...), custom_call_target="tpu_custom_call" | custom-call | flops 9200000000 | bytes 24000000 | tf_op jit(solution)/shard_map/qkv_own/pallas_call | solution.py:143
  35.6 3.0 collective-permute-start.1
  40.0 12.3 %halo.1 = (bf16[1792,768]{1,0:T(8,128)(2,1)}, bf16[1792,768]{1,0:T(8,128)(2,1)}, bf16[1792,768]{1,0:T(8,128)(2,1)}) custom-call(bf16[64,768]{1,0:T(8,128)(2,1)} %copy-done.45, bf16[512,768]{1,0:T(8,128)(2,1)} %collective-permute-done.4.near_l, ...), custom_call_target="tpu_custom_call", output_to_operand_aliasing={{0}: (9, {}), {1}: (10, {}), {2}: (11, {})} | custom-call | flops 13799999488 | bytes 36000000 | tf_op jit(solution)/shard_map/halo/pallas_call | solution.py:203
  52.3 8.1 %attention_forward.2 = (f32[512,768]{1,0:T(8,128)}, bf16[512,768]{1,0:T(8,128)(2,1)}, f32[3,4,1,512]{3,2,1,0:T(1,128)}) custom-call(s32[4,5]{1,0:T(4,128)} %stack.119.bound_ref, bf16[1792,768]{1,0:T(8,128)(2,1)} %get-tuple-element.132.q_ref, bf16[1792,768]{1,0:T(8,128)(2,1)} %get-tuple-element.133.k_ref, bf16[1792,768]{1,0:T(8,128)(2,1)} %get-tuple-element.134.v_ref, ...), custom_call_target="tpu_custom_call" | custom-call | flops 9200000000 | bytes 24000000 | tf_op jit(solution)/shard_map/attention_forward/pallas_call | solution.py:318
  63.1 9.8 %attention_forward.3 = (f32[512,768]{1,0:T(8,128)}, bf16[512,768]{1,0:T(8,128)(2,1)}, f32[3,4,1,512]{3,2,1,0:T(1,128)}) custom-call(s32[4,5]{1,0:T(4,128)} %stack.119.bound_ref, bf16[1792,768]{1,0:T(8,128)(2,1)} %get-tuple-element.132.q_ref, bf16[1792,768]{1,0:T(8,128)(2,1)} %get-tuple-element.133.k_ref, ...), custom_call_target="tpu_custom_call", output_to_operand_aliasing={{0}: (6, {}), {1}: (7, {}), {2}: (8, {})} | custom-call | flops 9200000000 | bytes 24000000 | tf_op jit(solution)/shard_map/attention_forward/pallas_call | solution.py:318
  73.0 11.6 %middle_own.1 = (f32[512,768]{1,0:T(8,128)}, bf16[512,768]{1,0:T(8,128)(2,1)}, f32[512,768]{1,0:T(8,128)}, f32[512,768]{1,0:T(8,128)}, f32[1,768]{1,0:T(1,128)},...) custom-call(s32[2]{0:T(128)} %pad_add_fusion.1.place_ref, bf16[512,768]{1,0:T(8,128)(2,1)} %bitcast.95, ...), custom_call_target="tpu_custom_call" | custom-call | flops 13799999488 | bytes 36000000 | tf_op jit(solution)/shard_map/middle_own/pallas_call | solution.py:622
  84.8 1.9 collective-permute-start.9
  87.4 9.5 %collective-permute-done.10.refs_3_ = bf16[3,192,768]{2,1,0:T(8,128)(2,1)S(1)} collective-permute-done((bf16[3,192,768]{2,1,0:T(8,128)(2,1)S(1)}, bf16[3,192,768]{2,1,0:T(8,128)(2,1)S(1)}, u32[]{:S(2)}, u32[]{:S(2)}) %collective-permute-start.10) | collective-permute-done | bytes 884768 | tf_op jit(solution)/shard_map/ppermute | solution.py:1048
  96.9 2.3 collective-permute-start.14
  99.4 2.5 add_convert_fusion.3
  104.0 21.0 %middle.1 = (bf16[512,768]{1,0:T(8,128)(2,1)}, f32[512,768]{1,0:T(8,128)}, bf16[560,768]{1,0:T(8,128)(2,1)S(1)}, bf16[80,768]{1,0:T(8,128)(2,1)S(1)}, bf16[80,76...) custom-call(s32[2]{0:T(128)S(1)} %copy-done.11, ...), custom_call_target="tpu_custom_call" | custom-call | flops 23000000512 | bytes 60000000 | tf_op jit(solution)/shard_map/middle/pallas_call | solution.py:787
  125.5 6.6 %collective-permute-start.16 = (bf16[560,768]{1,0:T(8,128)(2,1)S(1)}, bf16[560,768]{1,0:T(8,128)(2,1)S(1)}, u32[]{:S(2)}, u32[]{:S(2)}) collective-permute-start(bf16[560,768]{1,0:T(8,128)(2,1)S(1)} %get-tuple-element.165.do_ref), channel_id=1, source_target_pairs={{0,1},{1,2},{2,3},{4,5},{5,6},{6,7},{8,9},{9,10},{10,11},{12,13},{... | collective-permute-start | bytes 2580488 | tf_op jit(solution)/shard_map/ppermute | solution.py:1048
  133.4 3.7 %collective-permute-start.15 = (bf16[80,768]{1,0:T(8,128)(2,1)S(1)}, bf16[80,768]{1,0:T(8,128)(2,1)S(1)}, u32[]{:S(2)}, u32[]{:S(2)}) collective-permute-start(bf16[80,768]{1,0:T(8,128)(2,1)S(1)} %get-tuple-element.164), channel_id=1, source_target_pairs={{0,2},{1,3},{4,6},{5,7},{8,10},{9,11},{12,14},{13,15},{16,18},{17,... | collective-permute-start | bytes 368648 | tf_op jit(solution)/shard_map/ppermute | solution.py:1048
  138.6 2.8 add_convert_fusion
  141.5 1.5 collective-permute-start.21
  143.0 1.8 copy-done.14
  144.8 15.3 %attention_backward_own.1 = (f32[512,768]{1,0:T(8,128)S(1)}, f32[512,768]{1,0:T(8,128)S(1)}, f32[512,768]{1,0:T(8,128)S(1)}) custom-call(s32[4,5]{1,0:T(4,128)S(1)} %copy-done.7, bf16[1792,768]{1,0:T(8,128)(2,1)S(1)} %copy-done.12, bf16[560,768]{1,0:T(8,128)(2,1)S(1)} %get-tuple-element.165.do_ref, bf16[1792,768]{1,0:T(8,128)(2,1)S(1)} %copy-done.13, ...), custom_call_target="tpu_custom_call" | custom-call | flops 23000000512 | bytes 60000000 | tf_op jit(solution)/shard_map/attention_backward_own/pallas_call | solution.py:406
  161.4 6.4 %collective-permute-done.21 = bf16[2,672,768]{2,1,0:T(8,128)(2,1)S(1)} collective-permute-done((bf16[2,672,768]{2,1,0:T(8,128)(2,1)S(1)}, bf16[2,672,768]{2,1,0:T(8,128)(2,1)S(1)}, u32[]{:S(2)}, u32[]{:S(2)}) %collective-permute-start.21) | collective-permute-done | bytes 2064416 | tf_op jit(solution)/shard_map/ppermute | solution.py:1048
  167.8 2.7 fusion
  170.4 2.0 collective-permute-start.23
  172.5 6.8 %attention_backward_halo.1 = (f32[512,768]{1,0:T(8,128)S(1)}, f32[512,768]{1,0:T(8,128)S(1)}) custom-call(s32[14,2]{1,0:T(8,128)S(1)} %copy.93.bound_ref, bf16[1792,768]{1,0:T(8,128)(2,1)S(1)} %copy-done.12, bf16[80,768]{1,0:T(8,128)(2,1)S(1)} %collective-permute-done.15.far_l, bf16[560,768]{1,0:T(8,128)(2,1)S(1)} %collective-permute-done.16.near_l, ...), custom_call_target="tpu_custom_call" | custom-call | flops 12650000384 | bytes 33000000 | tf_op jit(solution)/shard_map/attention_backward_halo/pallas_call | solution.py:494
  179.3 5.4 %collective-permute-done.23 = bf16[672,768]{1,0:T(8,128)(2,1)S(1)} collective-permute-done((bf16[672,768]{1,0:T(8,128)(2,1)S(1)}, bf16[672,768]{1,0:T(8,128)(2,1)S(1)}, u32[]{:S(2)}, u32[]{:S(2)}) %collective-permute-start.23) | collective-permute-done | bytes 1032224 | tf_op jit(solution)/shard_map/ppermute | solution.py:1048
  184.8 2.2 fusion.4
  187.6 8.4 %turn_back.1 = (bf16[3,512,768]{2,1,0:T(8,128)(2,1)S(1)}, f32[3,768]{1,0:T(4,128)S(1)}, f32[8,384]{1,0:T(8,128)S(1)}, bf16[4,96,2304]{2,1,0:T(8,128)(2,1)S(1)}, bf16[4,96,2304]{2,1,0:T(8,128)(2,1)S(1)}) custom-call(s32[2]{0:T(128)S(1)} %copy-done.11, bf16[512,768]{1,0:T(8,128)(2,1)S(1)} %bitcast.96, f32[6,768]{1,0:T(8,128)S(1)} %copy-done.6, ...), custom_call_target="tpu_custom_call" | custom-call | flops 10350000128 | bytes 27000000 | tf_op jit(solution)/shard_map/turn_back/pallas_call | solution.py:880
  196.9 3.3 %collective-permute-done.24 = bf16[4,96,2304]{2,1,0:T(8,128)(2,1)S(1)} collective-permute-done((bf16[4,96,2304]{2,1,0:T(8,128)(2,1)S(1)}, bf16[4,96,2304]{2,1,0:T(8,128)(2,1)S(1)}, u32[]{:S(2)}, u32[]{:S(2)}) %collective-permute-start.24) | collective-permute-done | bytes 1769504 | tf_op jit(solution)/shard_map/ppermute | solution.py:1048
  200.4 1.8 collective-permute-start.25
  203.2 2.7 collective-permute-start.31
  206.1 4.4 %input_grad.1 = (f32[512,768]{1,0:T(8,128)}, f32[84,128]{1,0:T(8,128)S(1)}) custom-call(s32[2]{0:T(128)S(1)} %copy-done.11, bf16[512,768]{1,0:T(8,128)(2,1)S(1)} %bitcast.97, f32[6,768]{1,0:T(8,128)S(1)} %copy-done.6, bf16[3,512,768]{2,1,0:T(8,128)(2,1)S(1)} %get-tuple-element.195.d_ref, bf16[768,2304]{1,0:T(8,128)(2,1)S(1)} %copy-done.8, ...), custom_call_target="tpu_custom_call" | custom-call | flops 8049999872 | bytes 21000000 | tf_op jit(solution)/shard_map/input_grad/pallas_call | solution.py:942
  210.5 2.4 collective-permute-done.25
  213.1 1.8 collective-permute-start.26
  214.9 17.2 %collective-permute-done.31 = bf16[192,768]{1,0:T(8,128)(2,1)S(1)} collective-permute-done((bf16[192,768]{1,0:T(8,128)(2,1)S(1)}, bf16[192,768]{1,0:T(8,128)(2,1)S(1)}, u32[]{:S(2)}, u32[]{:S(2)}) %collective-permute-start.31) | collective-permute-done | bytes 294944 | tf_op jit(solution)/shard_map/ppermute | solution.py:1048
  241.8 2.3 collective-permute-start.29
  246.4 5.3 %collective-permute-done.28 = bf16[24,3072]{1,0:T(8,128)(2,1)S(1)} collective-permute-done((bf16[24,3072]{1,0:T(8,128)(2,1)S(1)}, bf16[24,3072]{1,0:T(8,128)(2,1)S(1)}, u32[]{:S(2)}, u32[]{:S(2)}) %collective-permute-start.28) | collective-permute-done | bytes 147488 | tf_op jit(solution)/shard_map/ppermute | solution.py:1048
  252.5 4.4 %collective-permute-start.36 = (bf16[24,3072]{1,0:T(8,128)(2,1)S(1)}, bf16[24,3072]{1,0:T(8,128)(2,1)S(1)}, u32[]{:S(2)}, u32[]{:S(2)}) collective-permute-start(bf16[24,3072]{1,0:T(8,128)(2,1)S(1)} %add_convert_fusion.6), channel_id=1, source_target_pairs={{0,1},{1,2},{2,3},{3,0},{4,5},{5,6},{6,7},{7,4},{8,9},{9,10},{10,1... | collective-permute-start | bytes 442376 | tf_op jit(solution)/shard_map/ppermute | solution.py:1048
  260.5 8.1 %collective-permute-done.37 = bf16[24,3072]{1,0:T(8,128)(2,1)S(1)} collective-permute-done((bf16[24,3072]{1,0:T(8,128)(2,1)S(1)}, bf16[24,3072]{1,0:T(8,128)(2,1)S(1)}, u32[]{:S(2)}, u32[]{:S(2)}) %collective-permute-start.37) | collective-permute-done | bytes 147488 | tf_op jit(solution)/shard_map/ppermute | solution.py:1048
  268.9 1.6 collective-permute-start.43
  270.4 1.5 collective-permute-start.44
  271.9 6.0 %collective-permute-done.39 = bf16[4,24,3072]{2,1,0:T(8,128)(2,1)S(1)} collective-permute-done((bf16[4,24,3072]{2,1,0:T(8,128)(2,1)S(1)}, bf16[4,24,3072]{2,1,0:T(8,128)(2,1)S(1)}, u32[]{:S(2)}, u32[]{:S(2)}) %collective-permute-start.39) | collective-permute-done | bytes 589856 | tf_op jit(solution)/shard_map/ppermute | solution.py:1048
  278.7 5.2 %assemble.2 = (f32[768,768]{1,0:T(8,128)}, f32[768,768]{1,0:T(8,128)}, f32[8,128]{1,0:T(8,128)S(1)}) custom-call(s32[2]{0:T(128)S(1)} %copy-done.11, bf16[2,192,768]{2,1,0:T(8,128)(2,1)S(1)} %pad_maximum_fusion.4.refs_0_, bf16[2,192,768]{2,1,0:T(8,128)(2,1)S(1)} %collective-permute-done.42.refs_1_, bf16[2,192,768]{2,1,0:T(8,128)(2,1)S(1)} %collective-permute-done.43.refs_2_, ...), custom_call_target="tpu_custom_call" | custom-call | flops 6899999744 | bytes 18000000 | tf_op jit(solution)/shard_map/assemble/pallas_call | solution.py:1031
  283.9 3.5 %collective-permute-start.45 = (f32[92,128]{1,0:T(8,128)S(1)}, f32[92,128]{1,0:T(8,128)S(1)}, u32[]{:S(2)}, u32[]{:S(2)}) collective-permute-start(f32[92,128]{1,0:T(8,128)S(1)} %pad_maximum_fusion.6), channel_id=1, source_target_pairs={{0,1},{1,0},{2,3},{3,2},{4,5},{5,4},{6,7},{7,6},{8,9},{9,8},{10,11... | collective-permute-start | bytes 141320 | tf_op jit(solution)/shard_map/ppermute | solution.py:1048
  287.4 1.8 collective-permute-done.45
  290.2 2.6 collective-permute-start.47
  293.4 2.7 collective-permute-start.48
  298.8 7.6 %assemble.3 = (f32[768,2304]{1,0:T(8,128)}, f32[768,768]{1,0:T(8,128)}, f32[8,128]{1,0:T(8,128)}, f32[2,128]{1,0:T(2,128)S(1)}) custom-call(s32[2]{0:T(128)S(1)} %copy-done.11, bf16[2,4,24,3072]{3,2,1,0:T(8,128)(2,1)S(1)} %pad_maximum_fusion.1.refs_0_, bf16[2,4,24,3072]{3,2,1,0:T(8,128)(2,1)S(1)} %collective-permute-done.40.refs_1_, ...), custom_call_target="tpu_custom_call" | custom-call | flops 6899999744 | bytes 18000000 | tf_op jit(solution)/shard_map/assemble/pallas_call | solution.py:1031
  (260 shorter events, 49.5 us)
Async XLA Ops:
  0.7 38.0 %collective-permute-start.4 = (bf16[512,768]{1,0:T(8,128)(2,1)}, bf16[512,768]{1,0:T(8,128)(2,1)}, u32[]{:S(2)}, u32[]{:S(2)}) collective-permute-start(bf16[512,768]{1,0:T(8,128)(2,1)} %bitcast.92), channel_id=1, source_target_pairs={{0,1},{1,2},{2,3},{4,5},{5,6},{6,7},{8,9},{9,10},{10,11},{12,13},{... | collective-permute-start | bytes 2359304 | tf_op jit(solution)/shard_map/ppermute | solution.py:1048
  5.8 33.0 %collective-permute-start.5 = (bf16[512,768]{1,0:T(8,128)(2,1)}, bf16[512,768]{1,0:T(8,128)(2,1)}, u32[]{:S(2)}, u32[]{:S(2)}) collective-permute-start(bf16[512,768]{1,0:T(8,128)(2,1)} %bitcast.93), channel_id=1, source_target_pairs={{1,0},{2,1},{3,2},{5,4},{6,5},{7,6},{9,8},{10,9},{11,10},{13,12},{... | collective-permute-start | bytes 2359304 | tf_op jit(solution)/shard_map/ppermute | solution.py:1048
  8.1 27.5 %collective-permute-start.3 = (bf16[64,768]{1,0:T(8,128)(2,1)S(1)}, bf16[64,768]{1,0:T(8,128)(2,1)S(1)}, u32[]{:S(2)}, u32[]{:S(2)}) collective-permute-start(bf16[64,768]{1,0:T(8,128)(2,1)S(1)} %get-tuple-element.324), channel_id=1, source_target_pairs={{0,2},{1,3},{4,6},{5,7},{8,10},{9,11},{12,14},{13,15},{16,18},{17,... | collective-permute-start | bytes 294920 | tf_op jit(solution)/shard_map/ppermute | solution.py:1048
  12.2 26.4 %collective-permute-start.6 = (bf16[64,768]{1,0:T(8,128)(2,1)S(1)}, bf16[64,768]{1,0:T(8,128)(2,1)S(1)}, u32[]{:S(2)}, u32[]{:S(2)}) collective-permute-start(bf16[64,768]{1,0:T(8,128)(2,1)S(1)} %get-tuple-element.323), channel_id=1, source_target_pairs={{2,0},{3,1},{6,4},{7,5},{10,8},{11,9},{14,12},{15,13},{18,16},{19,... | collective-permute-start | bytes 294920 | tf_op jit(solution)/shard_map/ppermute | solution.py:1048
  15.6 44.8 %collective-permute-start = (bf16[208,768]{1,0:T(8,128)(2,1)S(1)}, bf16[208,768]{1,0:T(8,128)(2,1)S(1)}, u32[]{:S(2)}, u32[]{:S(2)}) collective-permute-start(bf16[208,768]{1,0:T(8,128)(2,1)S(1)} %pad_maximum_fusion.5), channel_id=1, source_target_pairs={{0,1},{1,2},{2,3},{3,0},{4,5},{5,6},{6,7},{7,4},{8,9},{9,10},{10,1... | collective-permute-start | bytes 958472 | tf_op jit(solution)/shard_map/ppermute | solution.py:1048
  35.6 24.8 %collective-permute-start.1 = (bf16[208,768]{1,0:T(8,128)(2,1)S(1)}, bf16[208,768]{1,0:T(8,128)(2,1)S(1)}, u32[]{:S(2)}, u32[]{:S(2)}) collective-permute-start(bf16[208,768]{1,0:T(8,128)(2,1)S(1)} %pad_maximum_fusion.5), channel_id=1, source_target_pairs={{0,2},{1,3},{2,0},{3,1},{4,6},{5,7},{6,4},{7,5},{8,10},{9,11},{10,... | collective-permute-start | bytes 958472 | tf_op jit(solution)/shard_map/ppermute | solution.py:1048
  38.6 21.9 %collective-permute-start.2 = (bf16[208,768]{1,0:T(8,128)(2,1)S(1)}, bf16[208,768]{1,0:T(8,128)(2,1)S(1)}, u32[]{:S(2)}, u32[]{:S(2)}) collective-permute-start(bf16[208,768]{1,0:T(8,128)(2,1)S(1)} %pad_maximum_fusion.5), channel_id=1, source_target_pairs={{0,3},{1,0},{2,1},{3,2},{4,7},{5,4},{6,5},{7,6},{8,11},{9,8},{10,9... | collective-permute-start | bytes 958472 | tf_op jit(solution)/shard_map/ppermute | solution.py:1048
  60.6 24.0 %collective-permute-start.7 = (bf16[3,192,768]{2,1,0:T(8,128)(2,1)S(1)}, bf16[3,192,768]{2,1,0:T(8,128)(2,1)S(1)}, u32[]{:S(2)}, u32[]{:S(2)}) collective-permute-start(bf16[3,192,768]{2,1,0:T(8,128)(2,1)S(1)} %pad_maximum_fusion.2.refs_0_), channel_id=1, source_target_pairs={{0,8},{4,20},{8,0},{12,28},{16,24},{20,4},{24,16},{28,12},{1,9},{5... | collective-permute-start | bytes 2654216 | tf_op jit(solution)/shard_map/ppermute | solution.py:1048
  61.9 22.8 %collective-permute-start.8 = (bf16[3,192,768]{2,1,0:T(8,128)(2,1)S(1)}, bf16[3,192,768]{2,1,0:T(8,128)(2,1)S(1)}, u32[]{:S(2)}, u32[]{:S(2)}) collective-permute-start(bf16[3,192,768]{2,1,0:T(8,128)(2,1)S(1)} %pad_maximum_fusion.2.refs_0_), channel_id=1, source_target_pairs={{0,16},{4,12},{8,24},{12,4},{16,0},{20,28},{24,8},{28,20},{1,17},{... | collective-permute-start | bytes 2654216 | tf_op jit(solution)/shard_map/ppermute | solution.py:1048
  84.7 12.3 %collective-permute-start.10 = (bf16[3,192,768]{2,1,0:T(8,128)(2,1)S(1)}, bf16[3,192,768]{2,1,0:T(8,128)(2,1)S(1)}, u32[]{:S(2)}, u32[]{:S(2)}) collective-permute-start(bf16[3,192,768]{2,1,0:T(8,128)(2,1)S(1)} %collective-permute-done.7.refs_1_), channel_id=1, source_target_pairs={{0,16},{4,12},{8,24},{12,4},{16,0},{20,28},{24,8},{28,20},{1,17},{... | collective-permute-start | bytes 2654216 | tf_op jit(solution)/shard_map/ppermute | solution.py:1048
  84.8 14.6 %collective-permute-start.9 = (bf16[4,192,768]{2,1,0:T(8,128)(2,1)}, bf16[4,192,768]{2,1,0:T(8,128)(2,1)S(1)}, u32[]{:S(2)}, u32[]{:S(2)}) collective-permute-start(bf16[4,192,768]{2,1,0:T(8,128)(2,1)} %get-tuple-element.155), channel_id=1, source_target_pairs={{0,4},{4,0},{1,5},{5,1},{2,6},{6,2},{3,7},{7,3},{8,12},{12,8},{9,1... | collective-permute-start | bytes 3538952 | tf_op jit(solution)/shard_map/ppermute | solution.py:1048
  86.8 15.1 %collective-permute-start.11 = (bf16[3,192,768]{2,1,0:T(8,128)(2,1)S(1)}, bf16[3,192,768]{2,1,0:T(8,128)(2,1)S(1)}, u32[]{:S(2)}, u32[]{:S(2)}) collective-permute-start(bf16[3,192,768]{2,1,0:T(8,128)(2,1)S(1)} %pad_maximum_fusion.2.refs_0_), channel_id=1, source_target_pairs={{0,4},{4,0},{1,5},{5,1},{2,6},{6,2},{3,7},{7,3},{8,12},{12,8},{9,1... | collective-permute-start | bytes 2654216 | tf_op jit(solution)/shard_map/ppermute | solution.py:1048
  86.8 15.0 %collective-permute-start.12 = (bf16[3,192,768]{2,1,0:T(8,128)(2,1)S(1)}, bf16[3,192,768]{2,1,0:T(8,128)(2,1)S(1)}, u32[]{:S(2)}, u32[]{:S(2)}) collective-permute-start(bf16[3,192,768]{2,1,0:T(8,128)(2,1)S(1)} %collective-permute-done.7.refs_1_), channel_id=1, source_target_pairs={{0,4},{4,0},{1,5},{5,1},{2,6},{6,2},{3,7},{7,3},{8,12},{12,8},{9,1... | collective-permute-start | bytes 2654216 | tf_op jit(solution)/shard_map/ppermute | solution.py:1048
  87.3 14.5 %collective-permute-start.13 = (bf16[3,192,768]{2,1,0:T(8,128)(2,1)S(1)}, bf16[3,192,768]{2,1,0:T(8,128)(2,1)S(1)}, u32[]{:S(2)}, u32[]{:S(2)}) collective-permute-start(bf16[3,192,768]{2,1,0:T(8,128)(2,1)S(1)} %collective-permute-done.8.refs_2_), channel_id=1, source_target_pairs={{0,4},{4,0},{1,5},{5,1},{2,6},{6,2},{3,7},{7,3},{8,12},{12,8},{9,1... | collective-permute-start | bytes 2654216 | tf_op jit(solution)/shard_map/ppermute | solution.py:1048
  96.9 4.9 %collective-permute-start.14 = (bf16[3,192,768]{2,1,0:T(8,128)(2,1)S(1)}, bf16[3,192,768]{2,1,0:T(8,128)(2,1)S(1)}, u32[]{:S(2)}, u32[]{:S(2)}) collective-permute-start(bf16[3,192,768]{2,1,0:T(8,128)(2,1)S(1)} %collective-permute-done.10.refs_3_), channel_id=1, source_target_pairs={{0,4},{4,0},{1,5},{5,1},{2,6},{6,2},{3,7},{7,3},{8,12},{12,8},{9,1... | collective-permute-start | bytes 2654216 | tf_op jit(solution)/shard_map/ppermute | solution.py:1048
  125.0 12.1 %collective-permute-start.20 = (bf16[4,672,768]{2,1,0:T(8,128)(2,1)}, bf16[4,672,768]{2,1,0:T(8,128)(2,1)}, u32[]{:S(2)}, u32[]{:S(2)}) collective-permute-start(bf16[4,672,768]{2,1,0:T(8,128)(2,1)} %get-tuple-element.168), channel_id=1, source_target_pairs={{0,4},{4,0},{1,5},{5,1},{2,6},{6,2},{3,7},{7,3},{8,12},{12,8},{9,1... | collective-permute-start | bytes 12386312 | tf_op jit(solution)/shard_map/ppermute | solution.py:1048
  125.1 12.0 %collective-permute-start.19 = (bf16[2,192,768]{2,1,0:T(8,128)(2,1)}, bf16[2,192,768]{2,1,0:T(8,128)(2,1)}, u32[]{:S(2)}, u32[]{:S(2)}) collective-permute-start(bf16[2,192,768]{2,1,0:T(8,128)(2,1)} %add_convert_fusion.3), channel_id=1, source_target_pairs={{0,8},{4,20},{8,0},{12,28},{16,24},{20,4},{24,16},{28,12},{1,9},{5... | collective-permute-start | bytes 1769480 | tf_op jit(solution)/shard_map/ppermute | solution.py:1048
  125.5 46.9 %collective-permute-start.16 = (bf16[560,768]{1,0:T(8,128)(2,1)S(1)}, bf16[560,768]{1,0:T(8,128)(2,1)S(1)}, u32[]{:S(2)}, u32[]{:S(2)}) collective-permute-start(bf16[560,768]{1,0:T(8,128)(2,1)S(1)} %get-tuple-element.165.do_ref), channel_id=1, source_target_pairs={{0,1},{1,2},{2,3},{4,5},{5,6},{6,7},{8,9},{9,10},{10,11},{12,13},{... | collective-permute-start | bytes 2580488 | tf_op jit(solution)/shard_map/ppermute | solution.py:1048
  132.1 40.4 %collective-permute-start.17 = (bf16[560,768]{1,0:T(8,128)(2,1)S(1)}, bf16[560,768]{1,0:T(8,128)(2,1)S(1)}, u32[]{:S(2)}, u32[]{:S(2)}) collective-permute-start(bf16[560,768]{1,0:T(8,128)(2,1)S(1)} %get-tuple-element.165.do_ref), channel_id=1, source_target_pairs={{1,0},{2,1},{3,2},{5,4},{6,5},{7,6},{9,8},{10,9},{11,10},{13,12},{... | collective-permute-start | bytes 2580488 | tf_op jit(solution)/shard_map/ppermute | solution.py:1048
  133.4 39.1 %collective-permute-start.15 = (bf16[80,768]{1,0:T(8,128)(2,1)S(1)}, bf16[80,768]{1,0:T(8,128)(2,1)S(1)}, u32[]{:S(2)}, u32[]{:S(2)}) collective-permute-start(bf16[80,768]{1,0:T(8,128)(2,1)S(1)} %get-tuple-element.164), channel_id=1, source_target_pairs={{0,2},{1,3},{4,6},{5,7},{8,10},{9,11},{12,14},{13,15},{16,18},{17,... | collective-permute-start | bytes 368648 | tf_op jit(solution)/shard_map/ppermute | solution.py:1048
  138.5 21.6 %collective-permute-start.22 = (bf16[192,768]{1,0:T(8,128)(2,1)S(1)}, bf16[192,768]{1,0:T(8,128)(2,1)S(1)}, u32[]{:S(2)}, u32[]{:S(2)}) collective-permute-start(bf16[192,768]{1,0:T(8,128)(2,1)S(1)} %fusion.8), channel_id=1, source_target_pairs={{0,16},{4,12},{8,24},{12,4},{16,0},{20,28},{24,8},{28,20},{1,17},{... | collective-permute-start | bytes 884744 | tf_op jit(solution)/shard_map/ppermute | solution.py:1048
  141.5 26.3 %collective-permute-start.21 = (bf16[2,672,768]{2,1,0:T(8,128)(2,1)S(1)}, bf16[2,672,768]{2,1,0:T(8,128)(2,1)S(1)}, u32[]{:S(2)}, u32[]{:S(2)}) collective-permute-start(bf16[2,672,768]{2,1,0:T(8,128)(2,1)S(1)} %add_convert_fusion), channel_id=1, source_target_pairs={{0,8},{4,20},{8,0},{12,28},{16,24},{20,4},{24,16},{28,12},{1,9},{5... | collective-permute-start | bytes 6193160 | tf_op jit(solution)/shard_map/ppermute | solution.py:1048
  160.1 12.3 %collective-permute-start.18 = (bf16[80,768]{1,0:T(8,128)(2,1)S(1)}, bf16[80,768]{1,0:T(8,128)(2,1)S(1)}, u32[]{:S(2)}, u32[]{:S(2)}) collective-permute-start(bf16[80,768]{1,0:T(8,128)(2,1)S(1)} %get-tuple-element.166), channel_id=1, source_target_pairs={{2,0},{3,1},{6,4},{7,5},{10,8},{11,9},{14,12},{15,13},{18,16},{19,... | collective-permute-start | bytes 368648 | tf_op jit(solution)/shard_map/ppermute | solution.py:1048
  170.4 14.3 %collective-permute-start.23 = (bf16[672,768]{1,0:T(8,128)(2,1)S(1)}, bf16[672,768]{1,0:T(8,128)(2,1)S(1)}, u32[]{:S(2)}, u32[]{:S(2)}) collective-permute-start(bf16[672,768]{1,0:T(8,128)(2,1)S(1)} %fusion), channel_id=1, source_target_pairs={{0,16},{4,12},{8,24},{12,4},{16,0},{20,28},{24,8},{28,20},{1,17},{... | collective-permute-start | bytes 3096584 | tf_op jit(solution)/shard_map/ppermute | solution.py:1048
  196.0 4.2 %collective-permute-start.24 = (bf16[4,96,2304]{2,1,0:T(8,128)(2,1)S(1)}, bf16[4,96,2304]{2,1,0:T(8,128)(2,1)S(1)}, u32[]{:S(2)}, u32[]{:S(2)}) collective-permute-start(bf16[4,96,2304]{2,1,0:T(8,128)(2,1)S(1)} %get-tuple-element.194), channel_id=1, source_target_pairs={{0,4},{4,0},{1,5},{5,1},{2,6},{6,2},{3,7},{7,3},{8,12},{12,8},{9,1... | collective-permute-start | bytes 5308424 | tf_op jit(solution)/shard_map/ppermute | solution.py:1048
  200.4 12.5 %collective-permute-start.25 = (bf16[2,96,2304]{2,1,0:T(8,128)(2,1)S(1)}, bf16[2,96,2304]{2,1,0:T(8,128)(2,1)S(1)}, u32[]{:S(2)}, u32[]{:S(2)}) collective-permute-start(bf16[2,96,2304]{2,1,0:T(8,128)(2,1)S(1)} %add_convert_fusion.2), channel_id=1, source_target_pairs={{0,8},{4,20},{8,0},{12,28},{16,24},{20,4},{24,16},{28,12},{1,9},{5... | collective-permute-start | bytes 2654216 | tf_op jit(solution)/shard_map/ppermute | solution.py:1048
  202.2 12.7 %collective-permute-start.30 = (bf16[192,768]{1,0:T(8,128)(2,1)S(1)}, bf16[192,768]{1,0:T(8,128)(2,1)S(1)}, u32[]{:S(2)}, u32[]{:S(2)}) collective-permute-start(bf16[192,768]{1,0:T(8,128)(2,1)S(1)} %get-tuple-element.322), channel_id=1, source_target_pairs={{0,3},{1,0},{2,1},{3,2},{4,7},{5,4},{6,5},{7,6},{8,11},{9,8},{10,9... | collective-permute-start | bytes 884744 | tf_op jit(solution)/shard_map/ppermute | solution.py:1048
  203.2 29.0 %collective-permute-start.31 = (bf16[192,768]{1,0:T(8,128)(2,1)S(1)}, bf16[192,768]{1,0:T(8,128)(2,1)S(1)}, u32[]{:S(2)}, u32[]{:S(2)}) collective-permute-start(bf16[192,768]{1,0:T(8,128)(2,1)S(1)} %get-tuple-element.321), channel_id=1, source_target_pairs={{0,2},{1,3},{2,0},{3,1},{4,6},{5,7},{6,4},{7,5},{8,10},{9,11},{10,... | collective-permute-start | bytes 884744 | tf_op jit(solution)/shard_map/ppermute | solution.py:1048
  205.9 26.3 %collective-permute-start.32 = (bf16[192,768]{1,0:T(8,128)(2,1)S(1)}, bf16[192,768]{1,0:T(8,128)(2,1)S(1)}, u32[]{:S(2)}, u32[]{:S(2)}) collective-permute-start(bf16[192,768]{1,0:T(8,128)(2,1)S(1)} %get-tuple-element.320), channel_id=1, source_target_pairs={{0,1},{1,2},{2,3},{3,0},{4,5},{5,6},{6,7},{7,4},{8,9},{9,10},{10,1... | collective-permute-start | bytes 884744 | tf_op jit(solution)/shard_map/ppermute | solution.py:1048
  213.1 25.8 %collective-permute-start.26 = (bf16[96,2304]{1,0:T(8,128)(2,1)S(1)}, bf16[96,2304]{1,0:T(8,128)(2,1)}, u32[]{:S(2)}, u32[]{:S(2)}) collective-permute-start(bf16[96,2304]{1,0:T(8,128)(2,1)S(1)} %fusion.7), channel_id=1, source_target_pairs={{0,16},{4,12},{8,24},{12,4},{16,0},{20,28},{24,8},{28,20},{1,17},{... | collective-permute-start | bytes 1327112 | tf_op jit(solution)/shard_map/ppermute | solution.py:1048
  235.2 2.9 collective-permute-start.34
  238.1 7.5 %collective-permute-start.35 = (f32[84,128]{1,0:T(8,128)S(1)}, f32[84,128]{1,0:T(8,128)S(1)}, u32[]{:S(2)}, u32[]{:S(2)}) collective-permute-start(f32[84,128]{1,0:T(8,128)S(1)} %add.364), channel_id=1, source_target_pairs={{0,16},{16,0},{1,17},{17,1},{2,18},{18,2},{3,19},{19,3},{4,20},{20... | collective-permute-start | bytes 129032 | tf_op jit(solution)/shard_map/ppermute | solution.py:1048
  240.3 6.1 %collective-permute-start.27 = (bf16[24,3072]{1,0:T(8,128)(2,1)S(1)}, bf16[24,3072]{1,0:T(8,128)(2,1)S(1)}, u32[]{:S(2)}, u32[]{:S(2)}) collective-permute-start(bf16[24,3072]{1,0:T(8,128)(2,1)S(1)} %get-tuple-element.328), channel_id=1, source_target_pairs={{0,1},{1,2},{2,3},{3,0},{4,5},{5,6},{6,7},{7,4},{8,9},{9,10},{10,1... | collective-permute-start | bytes 442376 | tf_op jit(solution)/shard_map/ppermute | solution.py:1048
  240.4 11.2 %collective-permute-start.28 = (bf16[24,3072]{1,0:T(8,128)(2,1)S(1)}, bf16[24,3072]{1,0:T(8,128)(2,1)S(1)}, u32[]{:S(2)}, u32[]{:S(2)}) collective-permute-start(bf16[24,3072]{1,0:T(8,128)(2,1)S(1)} %get-tuple-element.329), channel_id=1, source_target_pairs={{0,2},{1,3},{2,0},{3,1},{4,6},{5,7},{6,4},{7,5},{8,10},{9,11},{10,... | collective-permute-start | bytes 442376 | tf_op jit(solution)/shard_map/ppermute | solution.py:1048
  241.8 9.8 %collective-permute-start.29 = (bf16[24,3072]{1,0:T(8,128)(2,1)S(1)}, bf16[24,3072]{1,0:T(8,128)(2,1)S(1)}, u32[]{:S(2)}, u32[]{:S(2)}) collective-permute-start(bf16[24,3072]{1,0:T(8,128)(2,1)S(1)} %get-tuple-element.327), channel_id=1, source_target_pairs={{0,3},{1,0},{2,1},{3,2},{4,7},{5,4},{6,5},{7,6},{8,11},{9,8},{10,9... | collective-permute-start | bytes 442376 | tf_op jit(solution)/shard_map/ppermute | solution.py:1048
  251.7 7.3 %collective-permute-start.41 = (bf16[192,768]{1,0:T(8,128)(2,1)S(1)}, bf16[192,768]{1,0:T(8,128)(2,1)S(1)}, u32[]{:S(2)}, u32[]{:S(2)}) collective-permute-start(bf16[192,768]{1,0:T(8,128)(2,1)S(1)} %fusion.3), channel_id=1, source_target_pairs={{0,8},{4,20},{8,0},{12,28},{16,24},{20,4},{24,16},{28,12},{1,9},{5... | collective-permute-start | bytes 884744 | tf_op jit(solution)/shard_map/ppermute | solution.py:1048
  252.5 8.0 %collective-permute-start.36 = (bf16[24,3072]{1,0:T(8,128)(2,1)S(1)}, bf16[24,3072]{1,0:T(8,128)(2,1)S(1)}, u32[]{:S(2)}, u32[]{:S(2)}) collective-permute-start(bf16[24,3072]{1,0:T(8,128)(2,1)S(1)} %add_convert_fusion.6), channel_id=1, source_target_pairs={{0,1},{1,2},{2,3},{3,0},{4,5},{5,6},{6,7},{7,4},{8,9},{9,10},{10,1... | collective-permute-start | bytes 442376 | tf_op jit(solution)/shard_map/ppermute | solution.py:1048
  256.9 11.7 %collective-permute-start.37 = (bf16[24,3072]{1,0:T(8,128)(2,1)S(1)}, bf16[24,3072]{1,0:T(8,128)(2,1)S(1)}, u32[]{:S(2)}, u32[]{:S(2)}) collective-permute-start(bf16[24,3072]{1,0:T(8,128)(2,1)S(1)} %add_convert_fusion.6), channel_id=1, source_target_pairs={{0,2},{1,3},{2,0},{3,1},{4,6},{5,7},{6,4},{7,5},{8,10},{9,11},{10,... | collective-permute-start | bytes 442376 | tf_op jit(solution)/shard_map/ppermute | solution.py:1048
  258.3 10.4 %collective-permute-start.38 = (bf16[24,3072]{1,0:T(8,128)(2,1)S(1)}, bf16[24,3072]{1,0:T(8,128)(2,1)S(1)}, u32[]{:S(2)}, u32[]{:S(2)}) collective-permute-start(bf16[24,3072]{1,0:T(8,128)(2,1)S(1)} %add_convert_fusion.6), channel_id=1, source_target_pairs={{0,3},{1,0},{2,1},{3,2},{4,7},{5,4},{6,5},{7,6},{8,11},{9,8},{10,9... | collective-permute-start | bytes 442376 | tf_op jit(solution)/shard_map/ppermute | solution.py:1048
  259.1 11.3 %collective-permute-start.42 = (bf16[2,192,768]{2,1,0:T(8,128)(2,1)S(1)}, bf16[2,192,768]{2,1,0:T(8,128)(2,1)S(1)}, u32[]{:S(2)}, u32[]{:S(2)}) collective-permute-start(bf16[2,192,768]{2,1,0:T(8,128)(2,1)S(1)} %pad_maximum_fusion.4.refs_0_), channel_id=1, source_target_pairs={{0,16},{4,12},{8,24},{12,4},{16,0},{20,28},{24,8},{28,20},{1,17},{... | collective-permute-start | bytes 1769480 | tf_op jit(solution)/shard_map/ppermute | solution.py:1048
  268.8 9.1 %collective-permute-start.39 = (bf16[4,24,3072]{2,1,0:T(8,128)(2,1)S(1)}, bf16[4,24,3072]{2,1,0:T(8,128)(2,1)S(1)}, u32[]{:S(2)}, u32[]{:S(2)}) collective-permute-start(bf16[4,24,3072]{2,1,0:T(8,128)(2,1)S(1)} %get-tuple-element.326), channel_id=1, source_target_pairs={{0,8},{4,20},{8,0},{12,28},{16,24},{20,4},{24,16},{28,12},{1,9},{5... | collective-permute-start | bytes 1769480 | tf_op jit(solution)/shard_map/ppermute | solution.py:1048
  268.9 9.8 %collective-permute-start.43 = (bf16[2,192,768]{2,1,0:T(8,128)(2,1)S(1)}, bf16[2,192,768]{2,1,0:T(8,128)(2,1)S(1)}, u32[]{:S(2)}, u32[]{:S(2)}) collective-permute-start(bf16[2,192,768]{2,1,0:T(8,128)(2,1)S(1)} %pad_maximum_fusion.4.refs_0_), channel_id=1, source_target_pairs={{0,4},{4,0},{1,5},{5,1},{2,6},{6,2},{3,7},{7,3},{8,12},{12,8},{9,1... | collective-permute-start | bytes 1769480 | tf_op jit(solution)/shard_map/ppermute | solution.py:1048
  270.4 8.3 %collective-permute-start.44 = (bf16[2,192,768]{2,1,0:T(8,128)(2,1)S(1)}, bf16[2,192,768]{2,1,0:T(8,128)(2,1)S(1)}, u32[]{:S(2)}, u32[]{:S(2)}) collective-permute-start(bf16[2,192,768]{2,1,0:T(8,128)(2,1)S(1)} %collective-permute-done.42.refs_1_), channel_id=1, source_target_pairs={{0,4},{4,0},{1,5},{5,1},{2,6},{6,2},{3,7},{7,3},{8,12},{12,8},{9,1... | collective-permute-start | bytes 1769480 | tf_op jit(solution)/shard_map/ppermute | solution.py:1048
  278.0 15.4 %collective-permute-start.40 = (bf16[2,4,24,3072]{3,2,1,0:T(8,128)(2,1)S(1)}, bf16[2,4,24,3072]{3,2,1,0:T(8,128)(2,1)S(1)}, u32[]{:S(2)}, u32[]{:S(2)}) collective-permute-start(bf16[2,4,24,3072]{3,2,1,0:T(8,128)(2,1)S(1)} %pad_maximum_fusion.1.refs_0_), channel_id=1, source_target_pairs={{0,16},{4,12},{8,24},{12,4},{16,0},{20,28},{24,8},{28,20},{1,17},{... | collective-permute-start | bytes 3538952 | tf_op jit(solution)/shard_map/ppermute | solution.py:1048
  283.9 5.3 %collective-permute-start.45 = (f32[92,128]{1,0:T(8,128)S(1)}, f32[92,128]{1,0:T(8,128)S(1)}, u32[]{:S(2)}, u32[]{:S(2)}) collective-permute-start(f32[92,128]{1,0:T(8,128)S(1)} %pad_maximum_fusion.6), channel_id=1, source_target_pairs={{0,1},{1,0},{2,3},{3,2},{4,5},{5,4},{6,7},{7,6},{8,9},{9,8},{10,11... | collective-permute-start | bytes 141320 | tf_op jit(solution)/shard_map/ppermute | solution.py:1048
  289.2 3.9 %collective-permute-start.46 = (f32[92,128]{1,0:T(8,128)S(1)}, f32[92,128]{1,0:T(8,128)S(1)}, u32[]{:S(2)}, u32[]{:S(2)}) collective-permute-start(f32[92,128]{1,0:T(8,128)S(1)} %fusion.39), channel_id=1, source_target_pairs={{0,2},{1,3},{2,0},{3,1},{4,6},{5,7},{6,4},{7,5},{8,10},{9,11},{10,... | collective-permute-start | bytes 141320 | tf_op jit(solution)/shard_map/ppermute | solution.py:1048
  290.2 8.5 %collective-permute-start.47 = (bf16[2,4,24,3072]{3,2,1,0:T(8,128)(2,1)S(1)}, bf16[2,4,24,3072]{3,2,1,0:T(8,128)(2,1)}, u32[]{:S(2)}, u32[]{:S(2)}) collective-permute-start(bf16[2,4,24,3072]{3,2,1,0:T(8,128)(2,1)S(1)} %pad_maximum_fusion.1.refs_0_), channel_id=1, source_target_pairs={{0,4},{4,0},{1,5},{5,1},{2,6},{6,2},{3,7},{7,3},{8,12},{12,8},{9,1... | collective-permute-start | bytes 3538952 | tf_op jit(solution)/shard_map/ppermute | solution.py:1048
  293.4 5.3 %collective-permute-start.48 = (bf16[2,4,24,3072]{3,2,1,0:T(8,128)(2,1)S(1)}, bf16[2,4,24,3072]{3,2,1,0:T(8,128)(2,1)}, u32[]{:S(2)}, u32[]{:S(2)}) collective-permute-start(bf16[2,4,24,3072]{3,2,1,0:T(8,128)(2,1)S(1)} %collective-permute-done.40.refs_1_), channel_id=1, source_target_pairs={{0,4},{4,0},{1,5},{5,1},{2,6},{6,2},{3,7},{7,3},{8,12},{12,8},{9,1... | collective-permute-start | bytes 3538952 | tf_op jit(solution)/shard_map/ppermute | solution.py:1048
  (49 other events, 401.2 us)
where the time goes:
time: 312 us; the launch traced here: 307 us
  Pallas kernels  119 us (38%)
  starting transfers between devices  77.8 us (25%)
  waiting for transfers between devices  69 us (22%)
  other arithmetic  22.8 us (7%)
  local copies, waits for them, and re-layouts  16 us (5%)
    ppermute x49, starting transfers between devices, send(): return lax.ppermute(x, axis, pairs)  77.8 us
    ppermute x49, waiting for transfers between devices, send(): return lax.ppermute(x, axis, pairs)  69 us
    pallas_call x1, Pallas kernels, middle_call(): pl.pallas_call(functools.partial(middle_kernel, slices=slices), in_specs=...  21 us
    pallas_call x2, Pallas kernels, forward_call(): pl.pallas_call(functools.partial(forward_kernel, first=first, base=base),...  17.9 us
    pallas_call x1, Pallas kernels, backward_own_call(): pl.pallas_call(functools.partial(backward_own_kernel, first=first), grid=...  15.3 us
    pallas_call x2, Pallas kernels, assemble_call(): pl.pallas_call(functools.partial(assemble_kernel, split=split, outs=len(s...  12.7 us
    pallas_call x1, Pallas kernels, halo_call(): pl.pallas_call(functools.partial(halo_kernel, which=which), grid=(4,), in...  12.3 us
    pallas_call x1, Pallas kernels, middle_own_call(): pl.pallas_call(functools.partial(middle_own_kernel, slices=slices), in_sp...  11.6 us
  transfers between devices with their start and end apart: 49, of which 16 were waited for; matrix products, arithmetic and copies ran while one was open for 10% of the time, Pallas kernels for 27%

commit v1 on v0

--- a/solution.py
+++ b/solution.py
@@ -1268,28 +1268,26 @@
         place, tokens, vectors, after(d_qkv, away), query_key_value_weight, d_hidden,
         grad_b_qkv, small_mid, freqs8, up_sum0, up_sums,
     )
-    got_1_qkv, small_in = lax.optimization_barrier((got_1_qkv, small_in))
     away = sum_low(kept_qkv[2], far_qkv[2], got_1_qkv[1]).astype(BF)
     got_2_qkv = send(away, PLANE, SECOND)
-    ff_got, small_in, _ = lax.optimization_barrier((ff_got, small_in, away))
     plane_qkv = wide_sum(sum_low(kept_qkv[0], far_qkv[0], got_1_qkv[0], got_2_qkv), extra)
-    ff_total = wide_sum(sum_low(kept_own[0], far_own[0], got_own[0][0], got_own[1]), extra)
-    ff_total = ff_total + sum_low(*ff_got)
 
     sizes = [width, width, 3 * width, width, rope_freqs.size] + [width] * 3 + [b_up.size * depth]
-    small = add_from(small_in, "c")
 
     part = plane_part((depth - 1) * rows, (depth - 1) * rows + width // slices)
     part = jnp.concatenate([plane_qkv, part], 1).astype(BF)
+    part, ff_got = lax.optimization_barrier((part, ff_got))
     thin = part.shape[0] // depth
     cut = lambda k: lax.dynamic_slice_in_dim(part, ((z + k) % depth) * thin, thin, 0)
     got = [send(cut(k), "n", ring(depth, k)) for k in range(1, depth)]
-    small = add_from(add_from(after(small, part), "b"), "a")
+    small = add_from(add_from(add_from(after(small_in, part), "c"), "b"), "a")
     if extra > 1:
         small = lax.psum(small, "e")
     got, small = lax.optimization_barrier((got, small))
     low = sum_low(cut(0), *got).astype(BF)
     strip = jnp.stack([low] + [send(low, "n", ring(depth, k)) for k in range(1, depth)])
+    ff_total = wide_sum(sum_low(kept_own[0], far_own[0], got_own[0][0], got_own[1]), extra)
+    ff_total = ff_total + sum_low(*ff_got)
     ff_pair, ff_last = plane_gather(after(ff_total, low).astype(BF))
     pair, last = plane_gather(strip)
     ff_pieces = [after(x, strip) for x in core_gather(ff_pair, ff_last)]

time: 312 us -> 307 us (0.984)
  starting transfers between devices: 77.8 us -> 90.1 us
  waiting for transfers between devices: 69 us -> 57.1 us
  other arithmetic: 22.8 us -> 19.6 us
    ppermute x49, starting transfers between devices: 77.8 us -> 90.1 us  [send(): return lax.ppermute(x, axis, pairs)]
    ppermute x49, waiting for transfers between devices: 69 us -> 57.1 us  [send(): return lax.ppermute(x, axis, pairs)]
    pallas_call x1, Pallas kernels: 15.3 us -> 18.6 us  [backward_own_call(): pl.pallas_call(functools.partial(backward_own_kernel, first=first), grid=...]
    unnamed x97 -> x85, local copies, waits for them, and re-layouts: 6.58 us -> 5.46 us
  transfers between devices with their start and end apart: 49 -> 49, of which waited for: 16 -> 16; matrix products, arithmetic and copies ran while one was open for 10% -> 9% of each run, Pallas kernels for 27% -> 27%
where the time goes in v1:
time: 307 us; the launch traced here: 302 us
  Pallas kernels  118 us (38%)
  starting transfers between devices  90.1 us (29%)
  waiting for transfers between devices  57.1 us (19%)
  other arithmetic  19.6 us (6%)
  local copies, waits for them, and re-layouts  15 us (5%)
    ppermute x49, starting transfers between devices, send(): return lax.ppermute(x, axis, pairs)  90.1 us
    ppermute x49, waiting for transfers between devices, send(): return lax.ppermute(x, axis, pairs)  57.1 us
    pallas_call x1, Pallas kernels, middle_call(): pl.pallas_call(functools.partial(middle_kernel, slices=slices), in_specs=...  21 us
    pallas_call x1, Pallas kernels, backward_own_call(): pl.pallas_call(functools.partial(backward_own_kernel, first=first), grid=...  18.6 us
    pallas_call x2, Pallas kernels, forward_call(): pl.pallas_call(functools.partial(forward_kernel, first=first, base=base),...  16.2 us
    pallas_call x2, Pallas kernels, assemble_call(): pl.pallas_call(functools.partial(assemble_kernel, split=split, outs=len(s...  12.7 us
    pallas_call x1, Pallas kernels, halo_call(): pl.pallas_call(functools.partial(halo_kernel, which=which), grid=(4,), in...  12.3 us
    pallas_call x1, Pallas kernels, middle_own_call(): pl.pallas_call(functools.partial(middle_own_kernel, slices=slices), in_sp...  11.7 us
  transfers between devices with their start and end apart: 49, of which 16 were waited for; matrix products, arithmetic and copies ran while one was open for 9% of the time, Pallas kernels for 27%

profile of v1, /device:TPU:1, one launch (start us, length us, event | category | flops | bytes accessed | tf_op | source)
XLA Modules:
  0.0 302.0 jit_solution(7241802701370642920)
XLA Ops:
  0.7 4.2 %collective-permute-start.4 = (bf16[512,768]{1,0:T(8,128)(2,1)}, bf16[512,768]{1,0:T(8,128)(2,1)S(1)}, u32[]{:S(2)}, u32[]{:S(2)}) collective-permute-start(bf16[512,768]{1,0:T(8,128)(2,1)} %bitcast.92), channel_id=1, source_target_pairs={{0,1},{1,2},{2,3},{4,5},{5,6},{6,7},{8,9},{9,10},{10,11},{12,13},{... | collective-permute-start | bytes 2359304 | tf_op jit(solution)/shard_map/ppermute | solution.py:1048
  7.2 5.0 %collective-permute-start.3 = (bf16[64,768]{1,0:T(8,128)(2,1)S(1)}, bf16[64,768]{1,0:T(8,128)(2,1)S(1)}, u32[]{:S(2)}, u32[]{:S(2)}) collective-permute-start(bf16[64,768]{1,0:T(8,128)(2,1)S(1)} %get-tuple-element.320), channel_id=1, source_target_pairs={{0,2},{1,3},{4,6},{5,7},{8,10},{9,11},{12,14},{13,15},{16,18},{17,... | collective-permute-start | bytes 294920 | tf_op jit(solution)/shard_map/ppermute | solution.py:1048
  15.6 2.3 collective-permute-start
  26.3 8.8 %qkv_own.1 = (bf16[1792,768]{1,0:T(8,128)(2,1)}, bf16[1792,768]{1,0:T(8,128)(2,1)}, bf16[1792,768]{1,0:T(8,128)(2,1)}, f32[512,768]{1,0:T(8,128)}, f32[512,768]{1,0:T(8,128)}, /*index=5*/bf16[768,2304]{1,0:T(8,128)(2,1)}) custom-call(bf16[512,768]{1,0:T(8,128)(2,1)} %bitcast.94, bf16[1792,128]{1,0:T(8,128)(2,1)} %fusion.1.hot_ref, f32[6,768]{1,0:T(8,128)} %stack.113.vec_ref, ...), custom_call_target="tpu_custom_call" | custom-call | flops 9200000000 | bytes 24000000 | tf_op jit(solution)/shard_map/qkv_own/pallas_call | solution.py:143
  35.6 3.0 collective-permute-start.1
  40.1 12.3 %halo.1 = (bf16[1792,768]{1,0:T(8,128)(2,1)}, bf16[1792,768]{1,0:T(8,128)(2,1)}, bf16[1792,768]{1,0:T(8,128)(2,1)}) custom-call(bf16[64,768]{1,0:T(8,128)(2,1)} %copy-done.39, bf16[512,768]{1,0:T(8,128)(2,1)} %copy-done.38, bf16[512,768]{1,0:T(8,128)(2,1)} %collective-permute-done.5.near_r, ...), custom_call_target="tpu_custom_call", output_to_operand_aliasing={{0}: (9, {}), {1}: (10, {}), {2}: (11, {})} | custom-call | flops 13799999488 | bytes 36000000 | tf_op jit(solution)/shard_map/halo/pallas_call | solution.py:203
  52.4 8.1 %attention_forward.2 = (f32[512,768]{1,0:T(8,128)}, bf16[512,768]{1,0:T(8,128)(2,1)}, f32[3,4,1,512]{3,2,1,0:T(1,128)}) custom-call(s32[4,5]{1,0:T(4,128)} %stack.119.bound_ref, bf16[1792,768]{1,0:T(8,128)(2,1)} %get-tuple-element.130.q_ref, bf16[1792,768]{1,0:T(8,128)(2,1)} %get-tuple-element.131.k_ref, bf16[1792,768]{1,0:T(8,128)(2,1)} %get-tuple-element.132.v_ref, ...), custom_call_target="tpu_custom_call" | custom-call | flops 9200000000 | bytes 24000000 | tf_op jit(solution)/shard_map/attention_forward/pallas_call | solution.py:318
  63.2 8.1 %attention_forward.3 = (f32[512,768]{1,0:T(8,128)}, bf16[512,768]{1,0:T(8,128)(2,1)}, f32[3,4,1,512]{3,2,1,0:T(1,128)}) custom-call(s32[4,5]{1,0:T(4,128)} %stack.119.bound_ref, bf16[1792,768]{1,0:T(8,128)(2,1)} %get-tuple-element.130.q_ref, bf16[1792,768]{1,0:T(8,128)(2,1)} %get-tuple-element.131.k_ref, ...), custom_call_target="tpu_custom_call", output_to_operand_aliasing={{0}: (6, {}), {1}: (7, {}), {2}: (8, {})} | custom-call | flops 9200000000 | bytes 24000000 | tf_op jit(solution)/shard_map/attention_forward/pallas_call | solution.py:318
  71.3 11.7 %middle_own.1 = (f32[512,768]{1,0:T(8,128)}, bf16[512,768]{1,0:T(8,128)(2,1)}, f32[512,768]{1,0:T(8,128)}, f32[512,768]{1,0:T(8,128)}, f32[1,768]{1,0:T(1,128)},...) custom-call(s32[2]{0:T(128)} %pad_add_fusion.1.place_ref, bf16[512,768]{1,0:T(8,128)(2,1)} %bitcast.95, ...), custom_call_target="tpu_custom_call" | custom-call | flops 13799999488 | bytes 36000000 | tf_op jit(solution)/shard_map/middle_own/pallas_call | solution.py:622
  83.0 2.1 collective-permute-start.10
  87.5 8.3 %collective-permute-done.10.refs_3_ = bf16[3,192,768]{2,1,0:T(8,128)(2,1)S(1)} collective-permute-done((bf16[3,192,768]{2,1,0:T(8,128)(2,1)S(1)}, bf16[3,192,768]{2,1,0:T(8,128)(2,1)S(1)}, u32[]{:S(2)}, u32[]{:S(2)}) %collective-permute-start.10) | collective-permute-done | bytes 884768 | tf_op jit(solution)/shard_map/ppermute | solution.py:1048
  95.8 3.8 %collective-permute-start.14 = (bf16[3,192,768]{2,1,0:T(8,128)(2,1)S(1)}, bf16[3,192,768]{2,1,0:T(8,128)(2,1)S(1)}, u32[]{:S(2)}, u32[]{:S(2)}) collective-permute-start(bf16[3,192,768]{2,1,0:T(8,128)(2,1)S(1)} %collective-permute-done.10.refs_3_), channel_id=1, source_target_pairs={{0,4},{4,0},{1,5},{5,1},{2,6},{6,2},{3,7},{7,3},{8,12},{12,8},{9,1... | collective-permute-start | bytes 2654216 | tf_op jit(solution)/shard_map/ppermute | solution.py:1048
  99.9 2.5 add_convert_fusion.3
  104.4 21.0 %middle.1 = (bf16[512,768]{1,0:T(8,128)(2,1)}, f32[512,768]{1,0:T(8,128)}, bf16[560,768]{1,0:T(8,128)(2,1)S(1)}, bf16[80,768]{1,0:T(8,128)(2,1)S(1)}, bf16[80,76...) custom-call(s32[2]{0:T(128)S(1)} %copy-done.11, ...), custom_call_target="tpu_custom_call" | custom-call | flops 23000000512 | bytes 60000000 | tf_op jit(solution)/shard_map/middle/pallas_call | solution.py:787
  125.8 8.4 %collective-permute-start.16 = (bf16[560,768]{1,0:T(8,128)(2,1)S(1)}, bf16[560,768]{1,0:T(8,128)(2,1)S(1)}, u32[]{:S(2)}, u32[]{:S(2)}) collective-permute-start(bf16[560,768]{1,0:T(8,128)(2,1)S(1)} %get-tuple-element.163.do_ref), channel_id=1, source_target_pairs={{0,1},{1,2},{2,3},{4,5},{5,6},{6,7},{8,9},{9,10},{10,11},{12,13},{... | collective-permute-start | bytes 2580488 | tf_op jit(solution)/shard_map/ppermute | solution.py:1048
  135.5 3.7 %collective-permute-start.15 = (bf16[80,768]{1,0:T(8,128)(2,1)S(1)}, bf16[80,768]{1,0:T(8,128)(2,1)S(1)}, u32[]{:S(2)}, u32[]{:S(2)}) collective-permute-start(bf16[80,768]{1,0:T(8,128)(2,1)S(1)} %get-tuple-element.162), channel_id=1, source_target_pairs={{0,2},{1,3},{4,6},{5,7},{8,10},{9,11},{12,14},{13,15},{16,18},{17,... | collective-permute-start | bytes 368648 | tf_op jit(solution)/shard_map/ppermute | solution.py:1048
  140.6 2.8 add_convert_fusion
  144.0 1.8 copy-done.14
  145.7 18.6 %attention_backward_own.1 = (f32[512,768]{1,0:T(8,128)S(1)}, f32[512,768]{1,0:T(8,128)S(1)}, f32[512,768]{1,0:T(8,128)S(1)}) custom-call(s32[4,5]{1,0:T(4,128)S(1)} %copy-done.7, bf16[1792,768]{1,0:T(8,128)(2,1)S(1)} %copy-done.12, bf16[560,768]{1,0:T(8,128)(2,1)S(1)} %get-tuple-element.163.do_ref, bf16[1792,768]{1,0:T(8,128)(2,1)S(1)} %copy-done.13, ...), custom_call_target="tpu_custom_call" | custom-call | flops 23000000512 | bytes 60000000 | tf_op jit(solution)/shard_map/attention_backward_own/pallas_call | solution.py:406
  165.7 2.6 collective-permute-done.21
  169.9 1.7 collective-permute-start.23
  172.7 4.0 %attention_backward_halo.1 = (f32[512,768]{1,0:T(8,128)S(1)}, f32[512,768]{1,0:T(8,128)S(1)}) custom-call(s32[14,2]{1,0:T(8,128)S(1)} %copy.93.bound_ref, bf16[1792,768]{1,0:T(8,128)(2,1)S(1)} %copy-done.12, bf16[80,768]{1,0:T(8,128)(2,1)S(1)} %collective-permute-done.15.far_l, bf16[560,768]{1,0:T(8,128)(2,1)S(1)} %collective-permute-done.16.near_l, ...), custom_call_target="tpu_custom_call" | custom-call | flops 12650000384 | bytes 33000000 | tf_op jit(solution)/shard_map/attention_backward_halo/pallas_call | solution.py:494
  176.7 7.3 %collective-permute-done.23 = bf16[672,768]{1,0:T(8,128)(2,1)S(1)} collective-permute-done((bf16[672,768]{1,0:T(8,128)(2,1)S(1)}, bf16[672,768]{1,0:T(8,128)(2,1)S(1)}, u32[]{:S(2)}, u32[]{:S(2)}) %collective-permute-start.23) | collective-permute-done | bytes 1032224 | tf_op jit(solution)/shard_map/ppermute | solution.py:1048
  184.0 1.7 fusion.4
  186.1 8.4 %turn_back.1 = (bf16[3,512,768]{2,1,0:T(8,128)(2,1)S(1)}, f32[3,768]{1,0:T(4,128)S(1)}, f32[8,384]{1,0:T(8,128)S(1)}, bf16[4,96,2304]{2,1,0:T(8,128)(2,1)S(1)}, bf16[4,96,2304]{2,1,0:T(8,128)(2,1)S(1)}) custom-call(s32[2]{0:T(128)S(1)} %copy-done.11, bf16[512,768]{1,0:T(8,128)(2,1)S(1)} %bitcast.96, f32[6,768]{1,0:T(8,128)S(1)} %copy-done.6, ...), custom_call_target="tpu_custom_call" | custom-call | flops 10350000128 | bytes 27000000 | tf_op jit(solution)/shard_map/turn_back/pallas_call | solution.py:880
  194.6 2.8 collective-permute-start.24
  197.4 3.3 %collective-permute-done.24 = bf16[4,96,2304]{2,1,0:T(8,128)(2,1)S(1)} collective-permute-done((bf16[4,96,2304]{2,1,0:T(8,128)(2,1)S(1)}, bf16[4,96,2304]{2,1,0:T(8,128)(2,1)S(1)}, u32[]{:S(2)}, u32[]{:S(2)}) %collective-permute-start.24) | collective-permute-done | bytes 1769504 | tf_op jit(solution)/shard_map/ppermute | solution.py:1048
  201.6 2.7 collective-permute-start.27
  204.3 4.3 %collective-permute-start.28 = (bf16[192,768]{1,0:T(8,128)(2,1)S(1)}, bf16[192,768]{1,0:T(8,128)(2,1)S(1)}, u32[]{:S(2)}, u32[]{:S(2)}) collective-permute-start(bf16[192,768]{1,0:T(8,128)(2,1)S(1)} %get-tuple-element.317), channel_id=1, source_target_pairs={{0,2},{1,3},{2,0},{3,1},{4,6},{5,7},{6,4},{7,5},{8,10},{9,11},{10,... | collective-permute-start | bytes 884744 | tf_op jit(solution)/shard_map/ppermute | solution.py:1048
  209.9 3.3 %collective-permute-done.25 = bf16[2,96,2304]{2,1,0:T(8,128)(2,1)S(1)} collective-permute-done((bf16[2,96,2304]{2,1,0:T(8,128)(2,1)S(1)}, bf16[2,96,2304]{2,1,0:T(8,128)(2,1)S(1)}, u32[]{:S(2)}, u32[]{:S(2)}) %collective-permute-start.25) | collective-permute-done | bytes 884768 | tf_op jit(solution)/shard_map/ppermute | solution.py:1048
  213.3 1.8 collective-permute-start.26
  215.1 4.4 %input_grad.1 = (f32[512,768]{1,0:T(8,128)}, f32[84,128]{1,0:T(8,128)S(1)}) custom-call(s32[2]{0:T(128)S(1)} %copy-done.11, bf16[512,768]{1,0:T(8,128)(2,1)S(1)} %bitcast.97, f32[6,768]{1,0:T(8,128)S(1)} %copy-done.6, bf16[3,512,768]{2,1,0:T(8,128)(2,1)S(1)} %get-tuple-element.193.d_ref, bf16[768,2304]{1,0:T(8,128)(2,1)S(1)} %copy-done.8, ...), custom_call_target="tpu_custom_call" | custom-call | flops 8049999872 | bytes 21000000 | tf_op jit(solution)/shard_map/input_grad/pallas_call | solution.py:942
  221.5 10.2 %collective-permute-done.28 = bf16[192,768]{1,0:T(8,128)(2,1)S(1)} collective-permute-done((bf16[192,768]{1,0:T(8,128)(2,1)S(1)}, bf16[192,768]{1,0:T(8,128)(2,1)S(1)}, u32[]{:S(2)}, u32[]{:S(2)}) %collective-permute-start.28) | collective-permute-done | bytes 294944 | tf_op jit(solution)/shard_map/ppermute | solution.py:1048
  234.4 2.3 collective-permute-start.32
  236.7 3.2 %collective-permute-start.35 = (f32[84,128]{1,0:T(8,128)S(1)}, f32[84,128]{1,0:T(8,128)S(1)}, u32[]{:S(2)}, u32[]{:S(2)}) collective-permute-start(f32[84,128]{1,0:T(8,128)S(1)} %add.364), channel_id=1, source_target_pairs={{0,16},{16,0},{1,17},{17,1},{2,18},{18,2},{3,19},{19,3},{4,20},{20... | collective-permute-start | bytes 129032 | tf_op jit(solution)/shard_map/ppermute | solution.py:1048
  241.7 4.2 %collective-permute-done.31 = bf16[24,3072]{1,0:T(8,128)(2,1)S(1)} collective-permute-done((bf16[24,3072]{1,0:T(8,128)(2,1)S(1)}, bf16[24,3072]{1,0:T(8,128)(2,1)S(1)}, u32[]{:S(2)}, u32[]{:S(2)}) %collective-permute-start.31) | collective-permute-done | bytes 147488 | tf_op jit(solution)/shard_map/ppermute | solution.py:1048
  246.0 3.2 %collective-permute-start.41 = (bf16[192,768]{1,0:T(8,128)(2,1)S(1)}, bf16[192,768]{1,0:T(8,128)(2,1)S(1)}, u32[]{:S(2)}, u32[]{:S(2)}) collective-permute-start(bf16[192,768]{1,0:T(8,128)(2,1)S(1)} %fusion.3), channel_id=1, source_target_pairs={{0,8},{4,20},{8,0},{12,28},{16,24},{20,4},{24,16},{28,12},{1,9},{5... | collective-permute-start | bytes 884744 | tf_op jit(solution)/shard_map/ppermute | solution.py:1048
  249.1 3.4 %collective-permute-start.36 = (bf16[24,3072]{1,0:T(8,128)(2,1)S(1)}, bf16[24,3072]{1,0:T(8,128)(2,1)S(1)}, u32[]{:S(2)}, u32[]{:S(2)}) collective-permute-start(bf16[24,3072]{1,0:T(8,128)(2,1)S(1)} %add_convert_fusion.6), channel_id=1, source_target_pairs={{0,1},{1,2},{2,3},{3,0},{4,5},{5,6},{6,7},{7,4},{8,9},{9,10},{10,1... | collective-permute-start | bytes 442376 | tf_op jit(solution)/shard_map/ppermute | solution.py:1048
  252.7 2.0 collective-permute-start.38
  256.3 6.9 %collective-permute-done.37 = bf16[24,3072]{1,0:T(8,128)(2,1)S(1)} collective-permute-done((bf16[24,3072]{1,0:T(8,128)(2,1)S(1)}, bf16[24,3072]{1,0:T(8,128)(2,1)S(1)}, u32[]{:S(2)}, u32[]{:S(2)}) %collective-permute-start.37) | collective-permute-done | bytes 147488 | tf_op jit(solution)/shard_map/ppermute | solution.py:1048
  264.5 3.2 %collective-permute-start.44 = (bf16[2,192,768]{2,1,0:T(8,128)(2,1)S(1)}, bf16[2,192,768]{2,1,0:T(8,128)(2,1)S(1)}, u32[]{:S(2)}, u32[]{:S(2)}) collective-permute-start(bf16[2,192,768]{2,1,0:T(8,128)(2,1)S(1)} %collective-permute-done.42.refs_1_), channel_id=1, source_target_pairs={{0,4},{4,0},{1,5},{5,1},{2,6},{6,2},{3,7},{7,3},{8,12},{12,8},{9,1... | collective-permute-start | bytes 1769480 | tf_op jit(solution)/shard_map/ppermute | solution.py:1048
  267.7 4.6 %collective-permute-done.39 = bf16[4,24,3072]{2,1,0:T(8,128)(2,1)S(1)} collective-permute-done((bf16[4,24,3072]{2,1,0:T(8,128)(2,1)S(1)}, bf16[4,24,3072]{2,1,0:T(8,128)(2,1)S(1)}, u32[]{:S(2)}, u32[]{:S(2)}) %collective-permute-start.39) | collective-permute-done | bytes 589856 | tf_op jit(solution)/shard_map/ppermute | solution.py:1048
  273.9 5.2 %assemble.2 = (f32[768,768]{1,0:T(8,128)}, f32[768,768]{1,0:T(8,128)}, f32[8,128]{1,0:T(8,128)S(1)}) custom-call(s32[2]{0:T(128)S(1)} %copy-done.11, bf16[2,192,768]{2,1,0:T(8,128)(2,1)S(1)} %pad_maximum_fusion.4.refs_0_, bf16[2,192,768]{2,1,0:T(8,128)(2,1)S(1)} %collective-permute-done.42.refs_1_, bf16[2,192,768]{2,1,0:T(8,128)(2,1)S(1)} %collective-permute-done.43.refs_2_, ...), custom_call_target="tpu_custom_call" | custom-call | flops 6899999744 | bytes 18000000 | tf_op jit(solution)/shard_map/assemble/pallas_call | solution.py:1031
  279.0 2.8 collective-permute-start.45
  281.9 1.8 collective-permute-done.45
  284.7 3.0 %collective-permute-start.47 = (bf16[2,4,24,3072]{3,2,1,0:T(8,128)(2,1)S(1)}, bf16[2,4,24,3072]{3,2,1,0:T(8,128)(2,1)}, u32[]{:S(2)}, u32[]{:S(2)}) collective-permute-start(bf16[2,4,24,3072]{3,2,1,0:T(8,128)(2,1)S(1)} %pad_maximum_fusion.refs_0_), channel_id=1, source_target_pairs={{0,4},{4,0},{1,5},{5,1},{2,6},{6,2},{3,7},{7,3},{8,12},{12,8},{9,1... | collective-permute-start | bytes 3538952 | tf_op jit(solution)/shard_map/ppermute | solution.py:1048
  287.9 3.1 %collective-permute-start.48 = (bf16[2,4,24,3072]{3,2,1,0:T(8,128)(2,1)S(1)}, bf16[2,4,24,3072]{3,2,1,0:T(8,128)(2,1)}, u32[]{:S(2)}, u32[]{:S(2)}) collective-permute-start(bf16[2,4,24,3072]{3,2,1,0:T(8,128)(2,1)S(1)} %collective-permute-done.40.refs_1_), channel_id=1, source_target_pairs={{0,4},{4,0},{1,5},{5,1},{2,6},{6,2},{3,7},{7,3},{8,12},{12,8},{9,1... | collective-permute-start | bytes 3538952 | tf_op jit(solution)/shard_map/ppermute | solution.py:1048
  293.7 7.6 %assemble.3 = (f32[768,2304]{1,0:T(8,128)}, f32[768,768]{1,0:T(8,128)}, f32[8,128]{1,0:T(8,128)}, f32[2,128]{1,0:T(2,128)S(1)}) custom-call(s32[2]{0:T(128)S(1)} %copy-done.11, bf16[2,4,24,3072]{3,2,1,0:T(8,128)(2,1)S(1)} %pad_maximum_fusion.refs_0_, bf16[2,4,24,3072]{3,2,1,0:T(8,128)(2,1)S(1)} %collective-permute-done.40.refs_1_, ...), custom_call_target="tpu_custom_call" | custom-call | flops 6899999744 | bytes 18000000 | tf_op jit(solution)/shard_map/assemble/pallas_call | solution.py:1031
  (249 shorter events, 48.4 us)
Async XLA Ops:
  0.7 38.1 %collective-permute-start.4 = (bf16[512,768]{1,0:T(8,128)(2,1)}, bf16[512,768]{1,0:T(8,128)(2,1)S(1)}, u32[]{:S(2)}, u32[]{:S(2)}) collective-permute-start(bf16[512,768]{1,0:T(8,128)(2,1)} %bitcast.92), channel_id=1, source_target_pairs={{0,1},{1,2},{2,3},{4,5},{5,6},{6,7},{8,9},{9,10},{10,11},{12,13},{... | collective-permute-start | bytes 2359304 | tf_op jit(solution)/shard_map/ppermute | solution.py:1048
  4.9 33.9 %collective-permute-start.5 = (bf16[512,768]{1,0:T(8,128)(2,1)}, bf16[512,768]{1,0:T(8,128)(2,1)}, u32[]{:S(2)}, u32[]{:S(2)}) collective-permute-start(bf16[512,768]{1,0:T(8,128)(2,1)} %bitcast.93), channel_id=1, source_target_pairs={{1,0},{2,1},{3,2},{5,4},{6,5},{7,6},{9,8},{10,9},{11,10},{13,12},{... | collective-permute-start | bytes 2359304 | tf_op jit(solution)/shard_map/ppermute | solution.py:1048
  7.2 28.4 %collective-permute-start.3 = (bf16[64,768]{1,0:T(8,128)(2,1)S(1)}, bf16[64,768]{1,0:T(8,128)(2,1)S(1)}, u32[]{:S(2)}, u32[]{:S(2)}) collective-permute-start(bf16[64,768]{1,0:T(8,128)(2,1)S(1)} %get-tuple-element.320), channel_id=1, source_target_pairs={{0,2},{1,3},{4,6},{5,7},{8,10},{9,11},{12,14},{13,15},{16,18},{17,... | collective-permute-start | bytes 294920 | tf_op jit(solution)/shard_map/ppermute | solution.py:1048
  12.2 26.4 %collective-permute-start.6 = (bf16[64,768]{1,0:T(8,128)(2,1)S(1)}, bf16[64,768]{1,0:T(8,128)(2,1)S(1)}, u32[]{:S(2)}, u32[]{:S(2)}) collective-permute-start(bf16[64,768]{1,0:T(8,128)(2,1)S(1)} %get-tuple-element.319), channel_id=1, source_target_pairs={{2,0},{3,1},{6,4},{7,5},{10,8},{11,9},{14,12},{15,13},{18,16},{19,... | collective-permute-start | bytes 294920 | tf_op jit(solution)/shard_map/ppermute | solution.py:1048
  15.6 44.9 %collective-permute-start = (bf16[208,768]{1,0:T(8,128)(2,1)S(1)}, bf16[208,768]{1,0:T(8,128)(2,1)S(1)}, u32[]{:S(2)}, u32[]{:S(2)}) collective-permute-start(bf16[208,768]{1,0:T(8,128)(2,1)S(1)} %pad_maximum_fusion.5), channel_id=1, source_target_pairs={{0,1},{1,2},{2,3},{3,0},{4,5},{5,6},{6,7},{7,4},{8,9},{9,10},{10,1... | collective-permute-start | bytes 958472 | tf_op jit(solution)/shard_map/ppermute | solution.py:1048
  35.6 24.9 %collective-permute-start.1 = (bf16[208,768]{1,0:T(8,128)(2,1)S(1)}, bf16[208,768]{1,0:T(8,128)(2,1)S(1)}, u32[]{:S(2)}, u32[]{:S(2)}) collective-permute-start(bf16[208,768]{1,0:T(8,128)(2,1)S(1)} %pad_maximum_fusion.5), channel_id=1, source_target_pairs={{0,2},{1,3},{2,0},{3,1},{4,6},{5,7},{6,4},{7,5},{8,10},{9,11},{10,... | collective-permute-start | bytes 958472 | tf_op jit(solution)/shard_map/ppermute | solution.py:1048
  38.6 21.9 %collective-permute-start.2 = (bf16[208,768]{1,0:T(8,128)(2,1)S(1)}, bf16[208,768]{1,0:T(8,128)(2,1)S(1)}, u32[]{:S(2)}, u32[]{:S(2)}) collective-permute-start(bf16[208,768]{1,0:T(8,128)(2,1)S(1)} %pad_maximum_fusion.5), channel_id=1, source_target_pairs={{0,3},{1,0},{2,1},{3,2},{4,7},{5,4},{6,5},{7,6},{8,11},{9,8},{10,9... | collective-permute-start | bytes 958472 | tf_op jit(solution)/shard_map/ppermute | solution.py:1048
  60.7 22.3 %collective-permute-start.7 = (bf16[3,192,768]{2,1,0:T(8,128)(2,1)S(1)}, bf16[3,192,768]{2,1,0:T(8,128)(2,1)S(1)}, u32[]{:S(2)}, u32[]{:S(2)}) collective-permute-start(bf16[3,192,768]{2,1,0:T(8,128)(2,1)S(1)} %pad_maximum_fusion.1.refs_0_), channel_id=1, source_target_pairs={{0,8},{4,20},{8,0},{12,28},{16,24},{20,4},{24,16},{28,12},{1,9},{5... | collective-permute-start | bytes 2654216 | tf_op jit(solution)/shard_map/ppermute | solution.py:1048
  62.0 21.0 %collective-permute-start.8 = (bf16[3,192,768]{2,1,0:T(8,128)(2,1)S(1)}, bf16[3,192,768]{2,1,0:T(8,128)(2,1)S(1)}, u32[]{:S(2)}, u32[]{:S(2)}) collective-permute-start(bf16[3,192,768]{2,1,0:T(8,128)(2,1)S(1)} %pad_maximum_fusion.1.refs_0_), channel_id=1, source_target_pairs={{0,16},{4,12},{8,24},{12,4},{16,0},{20,28},{24,8},{28,20},{1,17},{... | collective-permute-start | bytes 2654216 | tf_op jit(solution)/shard_map/ppermute | solution.py:1048
  83.0 12.8 %collective-permute-start.10 = (bf16[3,192,768]{2,1,0:T(8,128)(2,1)S(1)}, bf16[3,192,768]{2,1,0:T(8,128)(2,1)S(1)}, u32[]{:S(2)}, u32[]{:S(2)}) collective-permute-start(bf16[3,192,768]{2,1,0:T(8,128)(2,1)S(1)} %collective-permute-done.7.refs_1_), channel_id=1, source_target_pairs={{0,16},{4,12},{8,24},{12,4},{16,0},{20,28},{24,8},{28,20},{1,17},{... | collective-permute-start | bytes 2654216 | tf_op jit(solution)/shard_map/ppermute | solution.py:1048
  85.1 14.7 %collective-permute-start.9 = (bf16[4,192,768]{2,1,0:T(8,128)(2,1)}, bf16[4,192,768]{2,1,0:T(8,128)(2,1)S(1)}, u32[]{:S(2)}, u32[]{:S(2)}) collective-permute-start(bf16[4,192,768]{2,1,0:T(8,128)(2,1)} %get-tuple-element.153), channel_id=1, source_target_pairs={{0,4},{4,0},{1,5},{5,1},{2,6},{6,2},{3,7},{7,3},{8,12},{12,8},{9,1... | collective-permute-start | bytes 3538952 | tf_op jit(solution)/shard_map/ppermute | solution.py:1048
  86.9 15.4 %collective-permute-start.11 = (bf16[3,192,768]{2,1,0:T(8,128)(2,1)S(1)}, bf16[3,192,768]{2,1,0:T(8,128)(2,1)S(1)}, u32[]{:S(2)}, u32[]{:S(2)}) collective-permute-start(bf16[3,192,768]{2,1,0:T(8,128)(2,1)S(1)} %pad_maximum_fusion.1.refs_0_), channel_id=1, source_target_pairs={{0,4},{4,0},{1,5},{5,1},{2,6},{6,2},{3,7},{7,3},{8,12},{12,8},{9,1... | collective-permute-start | bytes 2654216 | tf_op jit(solution)/shard_map/ppermute | solution.py:1048
  86.9 15.4 %collective-permute-start.12 = (bf16[3,192,768]{2,1,0:T(8,128)(2,1)S(1)}, bf16[3,192,768]{2,1,0:T(8,128)(2,1)S(1)}, u32[]{:S(2)}, u32[]{:S(2)}) collective-permute-start(bf16[3,192,768]{2,1,0:T(8,128)(2,1)S(1)} %collective-permute-done.7.refs_1_), channel_id=1, source_target_pairs={{0,4},{4,0},{1,5},{5,1},{2,6},{6,2},{3,7},{7,3},{8,12},{12,8},{9,1... | collective-permute-start | bytes 2654216 | tf_op jit(solution)/shard_map/ppermute | solution.py:1048
  87.4 14.9 %collective-permute-start.13 = (bf16[3,192,768]{2,1,0:T(8,128)(2,1)S(1)}, bf16[3,192,768]{2,1,0:T(8,128)(2,1)S(1)}, u32[]{:S(2)}, u32[]{:S(2)}) collective-permute-start(bf16[3,192,768]{2,1,0:T(8,128)(2,1)S(1)} %collective-permute-done.8.refs_2_), channel_id=1, source_target_pairs={{0,4},{4,0},{1,5},{5,1},{2,6},{6,2},{3,7},{7,3},{8,12},{12,8},{9,1... | collective-permute-start | bytes 2654216 | tf_op jit(solution)/shard_map/ppermute | solution.py:1048
  95.8 6.5 %collective-permute-start.14 = (bf16[3,192,768]{2,1,0:T(8,128)(2,1)S(1)}, bf16[3,192,768]{2,1,0:T(8,128)(2,1)S(1)}, u32[]{:S(2)}, u32[]{:S(2)}) collective-permute-start(bf16[3,192,768]{2,1,0:T(8,128)(2,1)S(1)} %collective-permute-done.10.refs_3_), channel_id=1, source_target_pairs={{0,4},{4,0},{1,5},{5,1},{2,6},{6,2},{3,7},{7,3},{8,12},{12,8},{9,1... | collective-permute-start | bytes 2654216 | tf_op jit(solution)/shard_map/ppermute | solution.py:1048
  125.5 13.7 %collective-permute-start.20 = (bf16[4,672,768]{2,1,0:T(8,128)(2,1)}, bf16[4,672,768]{2,1,0:T(8,128)(2,1)}, u32[]{:S(2)}, u32[]{:S(2)}) collective-permute-start(bf16[4,672,768]{2,1,0:T(8,128)(2,1)} %get-tuple-element.166), channel_id=1, source_target_pairs={{0,4},{4,0},{1,5},{5,1},{2,6},{6,2},{3,7},{7,3},{8,12},{12,8},{9,1... | collective-permute-start | bytes 12386312 | tf_op jit(solution)/shard_map/ppermute | solution.py:1048
  125.5 13.6 %collective-permute-start.19 = (bf16[2,192,768]{2,1,0:T(8,128)(2,1)}, bf16[2,192,768]{2,1,0:T(8,128)(2,1)S(1)}, u32[]{:S(2)}, u32[]{:S(2)}) collective-permute-start(bf16[2,192,768]{2,1,0:T(8,128)(2,1)} %add_convert_fusion.3), channel_id=1, source_target_pairs={{0,8},{4,20},{8,0},{12,28},{16,24},{20,4},{24,16},{28,12},{1,9},{5... | collective-permute-start | bytes 1769480 | tf_op jit(solution)/shard_map/ppermute | solution.py:1048
  125.8 46.9 %collective-permute-start.16 = (bf16[560,768]{1,0:T(8,128)(2,1)S(1)}, bf16[560,768]{1,0:T(8,128)(2,1)S(1)}, u32[]{:S(2)}, u32[]{:S(2)}) collective-permute-start(bf16[560,768]{1,0:T(8,128)(2,1)S(1)} %get-tuple-element.163.do_ref), channel_id=1, source_target_pairs={{0,1},{1,2},{2,3},{4,5},{5,6},{6,7},{8,9},{9,10},{10,11},{12,13},{... | collective-permute-start | bytes 2580488 | tf_op jit(solution)/shard_map/ppermute | solution.py:1048
  134.2 38.5 %collective-permute-start.17 = (bf16[560,768]{1,0:T(8,128)(2,1)S(1)}, bf16[560,768]{1,0:T(8,128)(2,1)S(1)}, u32[]{:S(2)}, u32[]{:S(2)}) collective-permute-start(bf16[560,768]{1,0:T(8,128)(2,1)S(1)} %get-tuple-element.163.do_ref), channel_id=1, source_target_pairs={{1,0},{2,1},{3,2},{5,4},{6,5},{7,6},{9,8},{10,9},{11,10},{13,12},{... | collective-permute-start | bytes 2580488 | tf_op jit(solution)/shard_map/ppermute | solution.py:1048
  135.5 36.1 %collective-permute-start.15 = (bf16[80,768]{1,0:T(8,128)(2,1)S(1)}, bf16[80,768]{1,0:T(8,128)(2,1)S(1)}, u32[]{:S(2)}, u32[]{:S(2)}) collective-permute-start(bf16[80,768]{1,0:T(8,128)(2,1)S(1)} %get-tuple-element.162), channel_id=1, source_target_pairs={{0,2},{1,3},{4,6},{5,7},{8,10},{9,11},{12,14},{13,15},{16,18},{17,... | collective-permute-start | bytes 368648 | tf_op jit(solution)/shard_map/ppermute | solution.py:1048
  140.4 24.0 %collective-permute-start.22 = (bf16[192,768]{1,0:T(8,128)(2,1)S(1)}, bf16[192,768]{1,0:T(8,128)(2,1)S(1)}, u32[]{:S(2)}, u32[]{:S(2)}) collective-permute-start(bf16[192,768]{1,0:T(8,128)(2,1)S(1)} %fusion.8), channel_id=1, source_target_pairs={{0,16},{4,12},{8,24},{12,4},{16,0},{20,28},{24,8},{28,20},{1,17},{... | collective-permute-start | bytes 884744 | tf_op jit(solution)/shard_map/ppermute | solution.py:1048
  143.4 24.9 %collective-permute-start.21 = (bf16[2,672,768]{2,1,0:T(8,128)(2,1)S(1)}, bf16[2,672,768]{2,1,0:T(8,128)(2,1)S(1)}, u32[]{:S(2)}, u32[]{:S(2)}) collective-permute-start(bf16[2,672,768]{2,1,0:T(8,128)(2,1)S(1)} %add_convert_fusion), channel_id=1, source_target_pairs={{0,8},{4,20},{8,0},{12,28},{16,24},{20,4},{24,16},{28,12},{1,9},{5... | collective-permute-start | bytes 6193160 | tf_op jit(solution)/shard_map/ppermute | solution.py:1048
  164.4 8.2 %collective-permute-start.18 = (bf16[80,768]{1,0:T(8,128)(2,1)S(1)}, bf16[80,768]{1,0:T(8,128)(2,1)S(1)}, u32[]{:S(2)}, u32[]{:S(2)}) collective-permute-start(bf16[80,768]{1,0:T(8,128)(2,1)S(1)} %get-tuple-element.164), channel_id=1, source_target_pairs={{2,0},{3,1},{6,4},{7,5},{10,8},{11,9},{14,12},{15,13},{18,16},{19,... | collective-permute-start | bytes 368648 | tf_op jit(solution)/shard_map/ppermute | solution.py:1048
  169.9 14.0 %collective-permute-start.23 = (bf16[672,768]{1,0:T(8,128)(2,1)S(1)}, bf16[672,768]{1,0:T(8,128)(2,1)S(1)}, u32[]{:S(2)}, u32[]{:S(2)}) collective-permute-start(bf16[672,768]{1,0:T(8,128)(2,1)S(1)} %fusion), channel_id=1, source_target_pairs={{0,16},{4,12},{8,24},{12,4},{16,0},{20,28},{24,8},{28,20},{1,17},{... | collective-permute-start | bytes 3096584 | tf_op jit(solution)/shard_map/ppermute | solution.py:1048
  194.6 6.1 %collective-permute-start.24 = (bf16[4,96,2304]{2,1,0:T(8,128)(2,1)S(1)}, bf16[4,96,2304]{2,1,0:T(8,128)(2,1)S(1)}, u32[]{:S(2)}, u32[]{:S(2)}) collective-permute-start(bf16[4,96,2304]{2,1,0:T(8,128)(2,1)S(1)} %get-tuple-element.192), channel_id=1, source_target_pairs={{0,4},{4,0},{1,5},{5,1},{2,6},{6,2},{3,7},{7,3},{8,12},{12,8},{9,1... | collective-permute-start | bytes 5308424 | tf_op jit(solution)/shard_map/ppermute | solution.py:1048
  200.9 12.3 %collective-permute-start.25 = (bf16[2,96,2304]{2,1,0:T(8,128)(2,1)S(1)}, bf16[2,96,2304]{2,1,0:T(8,128)(2,1)S(1)}, u32[]{:S(2)}, u32[]{:S(2)}) collective-permute-start(bf16[2,96,2304]{2,1,0:T(8,128)(2,1)S(1)} %add_convert_fusion.2), channel_id=1, source_target_pairs={{0,8},{4,20},{8,0},{12,28},{16,24},{20,4},{24,16},{28,12},{1,9},{5... | collective-permute-start | bytes 2654216 | tf_op jit(solution)/shard_map/ppermute | solution.py:1048
  201.6 19.9 %collective-permute-start.27 = (bf16[192,768]{1,0:T(8,128)(2,1)S(1)}, bf16[192,768]{1,0:T(8,128)(2,1)S(1)}, u32[]{:S(2)}, u32[]{:S(2)}) collective-permute-start(bf16[192,768]{1,0:T(8,128)(2,1)S(1)} %get-tuple-element.318), channel_id=1, source_target_pairs={{0,3},{1,0},{2,1},{3,2},{4,7},{5,4},{6,5},{7,6},{8,11},{9,8},{10,9... | collective-permute-start | bytes 884744 | tf_op jit(solution)/shard_map/ppermute | solution.py:1048
  204.3 27.4 %collective-permute-start.28 = (bf16[192,768]{1,0:T(8,128)(2,1)S(1)}, bf16[192,768]{1,0:T(8,128)(2,1)S(1)}, u32[]{:S(2)}, u32[]{:S(2)}) collective-permute-start(bf16[192,768]{1,0:T(8,128)(2,1)S(1)} %get-tuple-element.317), channel_id=1, source_target_pairs={{0,2},{1,3},{2,0},{3,1},{4,6},{5,7},{6,4},{7,5},{8,10},{9,11},{10,... | collective-permute-start | bytes 884744 | tf_op jit(solution)/shard_map/ppermute | solution.py:1048
  208.6 23.1 %collective-permute-start.29 = (bf16[192,768]{1,0:T(8,128)(2,1)S(1)}, bf16[192,768]{1,0:T(8,128)(2,1)}, u32[]{:S(2)}, u32[]{:S(2)}) collective-permute-start(bf16[192,768]{1,0:T(8,128)(2,1)S(1)} %get-tuple-element.316), channel_id=1, source_target_pairs={{0,1},{1,2},{2,3},{3,0},{4,5},{5,6},{6,7},{7,4},{8,9},{9,10},{10,1... | collective-permute-start | bytes 884744 | tf_op jit(solution)/shard_map/ppermute | solution.py:1048
  213.3 7.9 %collective-permute-start.26 = (bf16[96,2304]{1,0:T(8,128)(2,1)S(1)}, bf16[96,2304]{1,0:T(8,128)(2,1)S(1)}, u32[]{:S(2)}, u32[]{:S(2)}) collective-permute-start(bf16[96,2304]{1,0:T(8,128)(2,1)S(1)} %fusion.7), channel_id=1, source_target_pairs={{0,16},{4,12},{8,24},{12,4},{16,0},{20,28},{24,8},{28,20},{1,17},{... | collective-permute-start | bytes 1327112 | tf_op jit(solution)/shard_map/ppermute | solution.py:1048
  233.0 3.8 %collective-permute-start.34 = (f32[84,128]{1,0:T(8,128)S(1)}, f32[84,128]{1,0:T(8,128)S(1)}, u32[]{:S(2)}, u32[]{:S(2)}) collective-permute-start(f32[84,128]{1,0:T(8,128)S(1)} %add.363), channel_id=1, source_target_pairs={{0,8},{8,0},{1,9},{9,1},{2,10},{10,2},{3,11},{11,3},{4,12},{12,4},... | collective-permute-start | bytes 129032 | tf_op jit(solution)/shard_map/ppermute | solution.py:1048
  233.1 8.6 %collective-permute-start.30 = (bf16[24,3072]{1,0:T(8,128)(2,1)S(1)}, bf16[24,3072]{1,0:T(8,128)(2,1)S(1)}, u32[]{:S(2)}, u32[]{:S(2)}) collective-permute-start(bf16[24,3072]{1,0:T(8,128)(2,1)S(1)} %get-tuple-element.325), channel_id=1, source_target_pairs={{0,1},{1,2},{2,3},{3,0},{4,5},{5,6},{6,7},{7,4},{8,9},{9,10},{10,1... | collective-permute-start | bytes 442376 | tf_op jit(solution)/shard_map/ppermute | solution.py:1048
  233.2 12.7 %collective-permute-start.31 = (bf16[24,3072]{1,0:T(8,128)(2,1)S(1)}, bf16[24,3072]{1,0:T(8,128)(2,1)S(1)}, u32[]{:S(2)}, u32[]{:S(2)}) collective-permute-start(bf16[24,3072]{1,0:T(8,128)(2,1)S(1)} %get-tuple-element.324), channel_id=1, source_target_pairs={{0,2},{1,3},{2,0},{3,1},{4,6},{5,7},{6,4},{7,5},{8,10},{9,11},{10,... | collective-permute-start | bytes 442376 | tf_op jit(solution)/shard_map/ppermute | solution.py:1048
  234.4 11.5 %collective-permute-start.32 = (bf16[24,3072]{1,0:T(8,128)(2,1)S(1)}, bf16[24,3072]{1,0:T(8,128)(2,1)S(1)}, u32[]{:S(2)}, u32[]{:S(2)}) collective-permute-start(bf16[24,3072]{1,0:T(8,128)(2,1)S(1)} %get-tuple-element.323), channel_id=1, source_target_pairs={{0,3},{1,0},{2,1},{3,2},{4,7},{5,4},{6,5},{7,6},{8,11},{9,8},{10,9... | collective-permute-start | bytes 442376 | tf_op jit(solution)/shard_map/ppermute | solution.py:1048
  236.7 5.0 %collective-permute-start.35 = (f32[84,128]{1,0:T(8,128)S(1)}, f32[84,128]{1,0:T(8,128)S(1)}, u32[]{:S(2)}, u32[]{:S(2)}) collective-permute-start(f32[84,128]{1,0:T(8,128)S(1)} %add.364), channel_id=1, source_target_pairs={{0,16},{16,0},{1,17},{17,1},{2,18},{18,2},{3,19},{19,3},{4,20},{20... | collective-permute-start | bytes 129032 | tf_op jit(solution)/shard_map/ppermute | solution.py:1048
  246.0 8.7 %collective-permute-start.41 = (bf16[192,768]{1,0:T(8,128)(2,1)S(1)}, bf16[192,768]{1,0:T(8,128)(2,1)S(1)}, u32[]{:S(2)}, u32[]{:S(2)}) collective-permute-start(bf16[192,768]{1,0:T(8,128)(2,1)S(1)} %fusion.3), channel_id=1, source_target_pairs={{0,8},{4,20},{8,0},{12,28},{16,24},{20,4},{24,16},{28,12},{1,9},{5... | collective-permute-start | bytes 884744 | tf_op jit(solution)/shard_map/ppermute | solution.py:1048
  249.1 7.1 %collective-permute-start.36 = (bf16[24,3072]{1,0:T(8,128)(2,1)S(1)}, bf16[24,3072]{1,0:T(8,128)(2,1)S(1)}, u32[]{:S(2)}, u32[]{:S(2)}) collective-permute-start(bf16[24,3072]{1,0:T(8,128)(2,1)S(1)} %add_convert_fusion.6), channel_id=1, source_target_pairs={{0,1},{1,2},{2,3},{3,0},{4,5},{5,6},{6,7},{7,4},{8,9},{9,10},{10,1... | collective-permute-start | bytes 442376 | tf_op jit(solution)/shard_map/ppermute | solution.py:1048
  252.6 10.5 %collective-permute-start.37 = (bf16[24,3072]{1,0:T(8,128)(2,1)S(1)}, bf16[24,3072]{1,0:T(8,128)(2,1)S(1)}, u32[]{:S(2)}, u32[]{:S(2)}) collective-permute-start(bf16[24,3072]{1,0:T(8,128)(2,1)S(1)} %add_convert_fusion.6), channel_id=1, source_target_pairs={{0,2},{1,3},{2,0},{3,1},{4,6},{5,7},{6,4},{7,5},{8,10},{9,11},{10,... | collective-permute-start | bytes 442376 | tf_op jit(solution)/shard_map/ppermute | solution.py:1048
  252.7 10.4 %collective-permute-start.38 = (bf16[24,3072]{1,0:T(8,128)(2,1)S(1)}, bf16[24,3072]{1,0:T(8,128)(2,1)S(1)}, u32[]{:S(2)}, u32[]{:S(2)}) collective-permute-start(bf16[24,3072]{1,0:T(8,128)(2,1)S(1)} %add_convert_fusion.6), channel_id=1, source_target_pairs={{0,3},{1,0},{2,1},{3,2},{4,7},{5,4},{6,5},{7,6},{8,11},{9,8},{10,9... | collective-permute-start | bytes 442376 | tf_op jit(solution)/shard_map/ppermute | solution.py:1048
  254.7 9.8 %collective-permute-start.42 = (bf16[2,192,768]{2,1,0:T(8,128)(2,1)S(1)}, bf16[2,192,768]{2,1,0:T(8,128)(2,1)S(1)}, u32[]{:S(2)}, u32[]{:S(2)}) collective-permute-start(bf16[2,192,768]{2,1,0:T(8,128)(2,1)S(1)} %pad_maximum_fusion.4.refs_0_), channel_id=1, source_target_pairs={{0,16},{4,12},{8,24},{12,4},{16,0},{20,28},{24,8},{28,20},{1,17},{... | collective-permute-start | bytes 1769480 | tf_op jit(solution)/shard_map/ppermute | solution.py:1048
  263.2 9.2 %collective-permute-start.39 = (bf16[4,24,3072]{2,1,0:T(8,128)(2,1)S(1)}, bf16[4,24,3072]{2,1,0:T(8,128)(2,1)S(1)}, u32[]{:S(2)}, u32[]{:S(2)}) collective-permute-start(bf16[4,24,3072]{2,1,0:T(8,128)(2,1)S(1)} %get-tuple-element.322), channel_id=1, source_target_pairs={{0,8},{4,20},{8,0},{12,28},{16,24},{20,4},{24,16},{28,12},{1,9},{5... | collective-permute-start | bytes 1769480 | tf_op jit(solution)/shard_map/ppermute | solution.py:1048
  263.3 10.6 %collective-permute-start.43 = (bf16[2,192,768]{2,1,0:T(8,128)(2,1)S(1)}, bf16[2,192,768]{2,1,0:T(8,128)(2,1)S(1)}, u32[]{:S(2)}, u32[]{:S(2)}) collective-permute-start(bf16[2,192,768]{2,1,0:T(8,128)(2,1)S(1)} %pad_maximum_fusion.4.refs_0_), channel_id=1, source_target_pairs={{0,4},{4,0},{1,5},{5,1},{2,6},{6,2},{3,7},{7,3},{8,12},{12,8},{9,1... | collective-permute-start | bytes 1769480 | tf_op jit(solution)/shard_map/ppermute | solution.py:1048
  264.5 9.3 %collective-permute-start.44 = (bf16[2,192,768]{2,1,0:T(8,128)(2,1)S(1)}, bf16[2,192,768]{2,1,0:T(8,128)(2,1)S(1)}, u32[]{:S(2)}, u32[]{:S(2)}) collective-permute-start(bf16[2,192,768]{2,1,0:T(8,128)(2,1)S(1)} %collective-permute-done.42.refs_1_), channel_id=1, source_target_pairs={{0,4},{4,0},{1,5},{5,1},{2,6},{6,2},{3,7},{7,3},{8,12},{12,8},{9,1... | collective-permute-start | bytes 1769480 | tf_op jit(solution)/shard_map/ppermute | solution.py:1048
  272.5 15.4 %collective-permute-start.40 = (bf16[2,4,24,3072]{3,2,1,0:T(8,128)(2,1)S(1)}, bf16[2,4,24,3072]{3,2,1,0:T(8,128)(2,1)S(1)}, u32[]{:S(2)}, u32[]{:S(2)}) collective-permute-start(bf16[2,4,24,3072]{3,2,1,0:T(8,128)(2,1)S(1)} %pad_maximum_fusion.refs_0_), channel_id=1, source_target_pairs={{0,16},{4,12},{8,24},{12,4},{16,0},{20,28},{24,8},{28,20},{1,17},{... | collective-permute-start | bytes 3538952 | tf_op jit(solution)/shard_map/ppermute | solution.py:1048
  279.0 4.6 %collective-permute-start.45 = (f32[92,128]{1,0:T(8,128)S(1)}, f32[92,128]{1,0:T(8,128)S(1)}, u32[]{:S(2)}, u32[]{:S(2)}) collective-permute-start(f32[92,128]{1,0:T(8,128)S(1)} %pad_maximum_fusion.6), channel_id=1, source_target_pairs={{0,1},{1,0},{2,3},{3,2},{4,5},{5,4},{6,7},{7,6},{8,9},{9,8},{10,11... | collective-permute-start | bytes 141320 | tf_op jit(solution)/shard_map/ppermute | solution.py:1048
  283.7 4.1 %collective-permute-start.46 = (f32[92,128]{1,0:T(8,128)S(1)}, f32[92,128]{1,0:T(8,128)S(1)}, u32[]{:S(2)}, u32[]{:S(2)}) collective-permute-start(f32[92,128]{1,0:T(8,128)S(1)} %fusion.35), channel_id=1, source_target_pairs={{0,2},{1,3},{2,0},{3,1},{4,6},{5,7},{6,4},{7,5},{8,10},{9,11},{10,... | collective-permute-start | bytes 141320 | tf_op jit(solution)/shard_map/ppermute | solution.py:1048
  284.7 8.9 %collective-permute-start.47 = (bf16[2,4,24,3072]{3,2,1,0:T(8,128)(2,1)S(1)}, bf16[2,4,24,3072]{3,2,1,0:T(8,128)(2,1)}, u32[]{:S(2)}, u32[]{:S(2)}) collective-permute-start(bf16[2,4,24,3072]{3,2,1,0:T(8,128)(2,1)S(1)} %pad_maximum_fusion.refs_0_), channel_id=1, source_target_pairs={{0,4},{4,0},{1,5},{5,1},{2,6},{6,2},{3,7},{7,3},{8,12},{12,8},{9,1... | collective-permute-start | bytes 3538952 | tf_op jit(solution)/shard_map/ppermute | solution.py:1048
  287.9 5.7 %collective-permute-start.48 = (bf16[2,4,24,3072]{3,2,1,0:T(8,128)(2,1)S(1)}, bf16[2,4,24,3072]{3,2,1,0:T(8,128)(2,1)}, u32[]{:S(2)}, u32[]{:S(2)}) collective-permute-start(bf16[2,4,24,3072]{3,2,1,0:T(8,128)(2,1)S(1)} %collective-permute-done.40.refs_1_), channel_id=1, source_target_pairs={{0,4},{4,0},{1,5},{5,1},{2,6},{6,2},{3,7},{7,3},{8,12},{12,8},{9,1... | collective-permute-start | bytes 3538952 | tf_op jit(solution)/shard_map/ppermute | solution.py:1048
  (43 other events, 392.3 us)
